TPU v7x, 256 devices: a whole 4x4x8 slice. The times are simulated.
256 devices in a mesh: row: 32 (over z, y), col: 8 (over x, core).
Axes of the slice: x: 4, y: 4, z: 8, core: 2. Of those that a mesh axis runs over, the one named last changes fastest.
Arguments:
- front_matrix: float32 [1, 32, 4, 8, 512, 512], P(None, 'row', None, 'col'), may hold values from -3 to 6, as said below
- block_map: int32 [64, 64], replicated, may hold values from 0 to 1, as said below
Outputs:
- factored: float32 [1, 32, 4, 8, 512, 512], P(None, 'row', None, 'col')
Inputs may be any that keep to these rules, and one draw needn't show every extreme that they name: front_matrix holds a symmetric front in the layout of the first step; multiplied by block_map it is positive definite. block_map is symmetric and 1 on the diagonal; two profile blocks that are both marked nonzero against a third are marked nonzero against each other.
All inputs are finite; a program needn't handle non-finite values.
Results may differ from a plain program's by a relative error of at most 0.0001.
Values sent between devices are 32-bit elements; how exact they have to be, the bound alone decides.
No kernel may reach another device: no remote copies, remote signals or barrier semaphores. Data moves between devices by JAX's collectives and lax.ppermute only.
A program may use at most 128 MiB of HBM per device.

v0:
```python
import jax
import jax.numpy as jnp
from jax import lax
from jax.sharding import PartitionSpec as P

BS = 256
PANELS = 1


HIGHEST_PRECISION = lax.Precision.HIGHEST


def spread(value, axis, source):
    kept = jnp.where(lax.axis_index(axis) == source, value, 0).astype(value.dtype)
    return lax.psum(kept, axis)


def right_solve(blocks, payload):
    number_blocks, block_width, _ = blocks.shape
    stacked = blocks.transpose(2, 0, 1).reshape(block_width, number_blocks * block_width)
    solved = lax.linalg.triangular_solve(payload, stacked, left_side=True, lower=True)
    return solved.reshape(block_width, number_blocks, block_width).transpose(1, 2, 0)


def body(front_matrix, block_map):
    row_blocks, _, col_blocks, _, block_width, _ = front_matrix.shape
    grid_rows = lax.axis_size("row")
    grid_cols = lax.axis_size("col")
    my_row = lax.axis_index("row")
    my_col = lax.axis_index("col")
    halves = block_width // BS
    local_map = block_map.reshape(row_blocks, grid_rows, halves, col_blocks, grid_cols, halves)
    local_map = lax.dynamic_index_in_dim(local_map, my_row, 1, keepdims=False)
    local_map = lax.dynamic_index_in_dim(local_map, my_col, 3, keepdims=False)
    weights = local_map.astype(jnp.float32).transpose(0, 2, 1, 3)
    working = (
        front_matrix.reshape(row_blocks, col_blocks, halves, BS, halves, BS)
        * weights[:, :, :, None, :, None]
    )
    working = working.reshape(row_blocks, col_blocks, block_width, block_width)
    row_ids = jnp.arange(row_blocks, dtype=jnp.int32) * grid_rows + my_row
    col_ids = jnp.arange(col_blocks, dtype=jnp.int32) * grid_cols + my_col
    identity = jnp.eye(block_width, dtype=jnp.float32)
    row_owner = 0 % grid_rows
    row_slot = 0 // grid_rows
    col_owner = 0 % grid_cols
    col_slot = 0 // grid_cols
    is_owner = jnp.logical_and(my_row == row_owner, my_col == col_owner)
    candidate = jnp.where(is_owner, working[row_slot, col_slot], identity)
    pivot_factor = jnp.linalg.cholesky(candidate)
    payload = pivot_factor
    payload = spread(payload, "col", col_owner)
    payload = spread(payload, "row", row_owner)
    column_raw = spread(working[:, col_slot], "col", col_owner)
    row_factor = right_solve(column_raw, payload)
    row_factor = jnp.where((row_ids >= 0)[:, None, None], row_factor, 0.0)
    pieces = []
    for member in range(grid_rows // grid_cols):
        pieces.append(spread(row_factor, "row", member * grid_cols + my_col))
    col_factor = jnp.stack(pieces, 1).reshape(col_blocks, block_width, block_width)
    row_update = jnp.where((row_ids > 0)[:, None, None], row_factor, 0.0)
    col_update = jnp.where((col_ids > 0)[:, None, None], col_factor, 0.0)
    working = working - jnp.einsum(
        "axk,cyk->acxy",
        row_update,
        col_update,
        precision=HIGHEST_PRECISION,
        preferred_element_type=jnp.float32,
    )
    panels = (col_owner, col_slot, row_factor)
    col_owner, col_slot, row_factor = panels
    holder = my_col == col_owner
    working = working.at[:, col_slot].set(jnp.where(holder, row_factor, working[:, col_slot]))
    keeping = jnp.logical_or((row_ids >= PANELS)[:, None], (col_ids < PANELS)[None, :])
    return jnp.where(keeping[:, :, None, None], working, 0.0).reshape(front_matrix.shape)


def solution(mesh):
    return jax.shard_map(
        body,
        mesh=mesh,
        in_specs=(P(None, "row", None, "col", None, None), P()),
        out_specs=P(None, "row", None, "col", None, None),
        check_vma=False,
    )
```

profile of v0, /device:TPU:10, one launch (start us, length us, event | category | flops | bytes accessed | tf_op | source)
XLA Modules:
  0.0 587.0 jit_solution(15624583379820426808)
XLA Ops:
  6.5 1.8 reshape.214
  8.4 0.1 copy.27
  8.5 0.1 copy.19
  8.6 3.2 mul.35
  11.8 6.4 %mul.36 = f32[1,4,512,512]{2,3,1,0:T(8,128)} reshape(f32[4,2,256,2,256]{2,1,4,3,0:T(2,128)} %mul.35) | data formatting | bytes 8388608 | tf_op jit(solution)/shard_map/mul | solution.py:37
  18.2 5.7 copy.17
  23.9 6.5 %bitcast_multiply_fusion = f32[1,4,512,512]{2,3,1,0:T(8,128)} fusion(f32[1,4,512,512]{2,3,1,0:T(8,128)} %mul.36, f32[1,1,4,1,512,512]{4,5,2,3,1,0:T(8,128)} %copy.17), kind=kLoop, calls=%fused_computation.11 | loop fusion | flops 1048576 | bytes 12582912 | tf_op jit(solution)/shard_map/mul | solution.py:37
  30.4 2.3 select_bitcast_fusion.1
  32.7 1.3 bitcast_select_fusion
  34.1 0.3 copy.20
  34.4 1.5 fusion.14
  35.9 11.7 %cholesky.104 = f32[128,128]{1,0:T(8,128)S(1)} custom-call(f32[128,128]{1,0:T(8,128)S(1)} %cholesky.266), custom_call_target="Cholesky" | custom-call | tf_op jit(solution)/shard_map/jit(cholesky)/cholesky | solution.py:50
  47.6 0.1 cholesky.224
  47.8 9.8 %custom-call.30 = f32[1,128,128]{1,2,0:T(8,128)S(1)} custom-call(f32[1,128,128]{2,1,0:T(8,128)S(1)} %get-tuple-element.53), custom_call_target="InvertDiagBlocksLowerTriangular" | custom-call | tf_op jit(solution)/shard_map/jit(cholesky)/cholesky | solution.py:50
  57.6 0.3 constant_dynamic-update-slice_fusion.3
  57.9 0.3 convolution_subtract_fusion.3
  58.2 11.8 %cholesky.217 = f32[128,128]{1,0:T(8,128)S(1)} custom-call(f32[128,128]{1,0:T(8,128)S(1)} %cholesky.270), custom_call_target="Cholesky" | custom-call | tf_op jit(solution)/shard_map/jit(cholesky)/cholesky | solution.py:50
  70.1 9.8 %custom-call.31 = f32[1,128,128]{1,2,0:T(8,128)S(1)} custom-call(f32[1,128,128]{2,1,0:T(8,128)S(1)} %get-tuple-element.50), custom_call_target="InvertDiagBlocksLowerTriangular" | custom-call | tf_op jit(solution)/shard_map/jit(cholesky)/cholesky | solution.py:50
  79.9 0.3 convolution_dynamic-update-slice_fusion
  80.2 0.4 convolution_subtract_fusion.4
  80.6 11.7 %cholesky.238 = f32[128,128]{1,0:T(8,128)S(1)} custom-call(f32[128,128]{1,0:T(8,128)S(1)} %cholesky.275), custom_call_target="Cholesky" | custom-call | tf_op jit(solution)/shard_map/jit(cholesky)/cholesky | solution.py:50
  92.4 0.7 compare_reduce_fusion.1
  93.1 9.8 %custom-call.32 = f32[1,128,128]{1,2,0:T(8,128)S(1)} custom-call(f32[1,128,128]{2,1,0:T(8,128)S(1)} %get-tuple-element.47), custom_call_target="InvertDiagBlocksLowerTriangular" | custom-call | tf_op jit(solution)/shard_map/jit(cholesky)/cholesky | solution.py:50
  102.9 0.2 convolution_dynamic-update-slice_fusion.1
  103.1 0.4 convolution_subtract_fusion.5
  103.5 11.9 %cholesky.255 = f32[128,128]{1,0:T(8,128)S(1)} custom-call(f32[128,128]{1,0:T(8,128)S(1)} %convolution_subtract_fusion.5), custom_call_target="Cholesky" | custom-call | tf_op jit(solution)/shard_map/jit(cholesky)/cholesky | solution.py:50
  115.4 0.6 compare_reduce_fusion
  116.1 0.7 compare_reduce_fusion.2
  119.3 1.1 select_select_fusion
  120.5 0.0 all-reduce.7.cloned.1.call-start
  120.5 71.4 %all-reduce.11.cloned.1.call-done = (f32[512,1,512]{2,0,1:T(8,128)}, f32[512,512]{1,0:T(8,128)}) async-done(((f32[512,1,512]{2,0,1:T(8,128)}, f32[512,512]{1,0:T(8,128)}), (f32[512,1,512]{2,0,1:T(8,128)}, f32[512,512]{1,0:T(8,128)})) %all-reduce.11.cloned.1.call-update) | async-done | bytes 2097168 | tf_op jit(solution)/shard_map/psum | solution.py:15
  191.9 1.1 broadcast_select_fusion.4
  193.0 0.0 all-reduce.7.cloned.1.call-update
  193.0 0.0 all-reduce.9.cloned.1.call-start
  193.1 152.5 %all-reduce.7.cloned.1.call-done = f32[512,512]{1,0:T(8,128)} async-done(((f32[512,512]{1,0:T(8,128)}), f32[512,512]{1,0:T(8,128)}) %all-reduce.7.cloned.1.call-update) | async-done | bytes 1048592 | tf_op jit(solution)/shard_map/psum | solution.py:15
  345.6 1.3 fusion.16
  347.0 8.1 %while.2 = (s32[]{:T(128)}, f32[512,512]{1,0:T(8,128)S(1)}, s32[4,2]{0,1:T(2,128)S(1)}, f32[4,128,128]{2,1,0:T(8,128)S(1)}, s32[]{:T(128)}) while((s32[]{:T(128)}, f32[512,512]{1,0:T(8,128)S(1)}, s32[4,2]{0,1:T(2,128)S(1)}, f32[4,128,128]{2,1,0:T(8,128)S(1)}, s32[]{:T(128)}) %tuple.34), condition=%wide.while_cond.1, body=%wide.while_body.1.sunk | while | flops 2 | bytes 131181 | solution.py:21
  347.0 0.1 constant_dynamic-slice_fusion.3
  347.1 0.6 fusion.58
  347.7 1.3 bitcast_dynamic-update-slice_fusion.2
  349.0 0.1 constant_dynamic-slice_fusion.3
  349.1 0.6 fusion.58
  349.7 1.3 bitcast_dynamic-update-slice_fusion.2
  351.1 0.1 constant_dynamic-slice_fusion.3
  351.2 0.6 fusion.58
  351.7 1.3 bitcast_dynamic-update-slice_fusion.2
  353.1 0.1 constant_dynamic-slice_fusion.3
  353.2 0.6 fusion.58
  353.8 1.3 bitcast_dynamic-update-slice_fusion.2
  355.1 39.3 %custom-call.33 = f32[4,128,128]{1,2,0:T(8,128)S(1)} custom-call(f32[4,128,128]{2,1,0:T(8,128)S(1)} %get-tuple-element.24), custom_call_target="InvertDiagBlocksLowerTriangular" | custom-call | tf_op jit(solution)/shard_map/triangular_solve | solution.py:21
  394.5 0.4 fusion.27
  394.9 0.4 convolution_subtract_fusion.1
  395.3 0.4 fusion.39
  395.7 0.4 convolution_subtract_fusion
  396.1 0.4 fusion.37
  396.6 0.6 convolution_subtract_fusion.2
  397.2 0.4 fusion.36
  397.6 1.1 broadcast_select_fusion
  398.7 1.9 broadcast_select_fusion.3
  400.6 162.1 %all-reduce.9.cloned.1.call-done = (f32[1,512,512]{1,2,0:T(8,128)}, f32[1,512,512]{1,2,0:T(8,128)}, f32[1,512,512]{1,2,0:T(8,128)}, f32[1,512,512]{1,2,0:T(8,128)}) async-done(((f32[1,512,512]{1,2,0:T(8,128)}, f32[1,512,512]{1,2,0:T(8,128)}, f32[1,512,512]{1,2,0:T(8,128)}, f32[1,512,512]{1,2,0:T(8,128)}), (f32[1,512,512]{1,2,0:T(8,128)}, f32[1,512,512]{1,2,0:T(8,128)}, f32[1,512,512]{1,2,0:T(8,128)}, ...) | async-done | bytes 4194320 | tf_op jit(solution)/shard_map/psum | solution.py:15
  562.8 9.4 %bitcast_subtract_fusion = f32[1,4,512,512]{2,3,1,0:T(8,128)S(1)} fusion(f32[1,4,512,512]{2,3,1,0:T(8,128)} %bitcast_multiply_fusion, f32[1,512,512]{1,2,0:T(8,128)} %get-tuple-element.33, f32[1,512,512]{1,2,0:T(8,128)} %get-tuple-element.34, f32[1,512,512]{1,2,0:T(8,128)} %get-tuple-element.35, f32[1,512,512]{1,2,0:T(8,128)} %get-tuple-element.36, ...), kind=kOutput, calls=%fused_computation.10 | convolution fusion | flops 6449004544 | bytes 13631494 | tf_op jit(solution)/shard_map/axk,cyk->acxy/dot_general | solution.py:63
  572.2 0.3 fusion.11
  572.5 2.5 select_bitcast_fusion
  575.0 5.2 copy.23
  (18 shorter events, 0.2 us)
Async XLA Ops:
  6.5 185.4 %all-reduce.11.cloned.1.call-start = ((), (), s32[]{:S(2)}) async-start(), calls=%async_computation.2 | async-start | bytes 4194304 | tf_op jit(solution)/shard_map/psum | solution.py:15
  120.5 225.2 %all-reduce.7.cloned.1.call-start = ((), (), s32[]{:S(2)}) async-start(), calls=%async_computation | async-start | bytes 2097152 | tf_op jit(solution)/shard_map/psum | solution.py:15
  191.9 202.6 %copy-start = (f32[512,1,512]{2,0,1:T(8,128)S(1)}, f32[512,1,512]{2,0,1:T(8,128)}, u32[]{:S(2)}) copy-start(f32[512,1,512]{2,0,1:T(8,128)} %get-tuple-element.37) | copy-start | bytes 3145732
  193.0 369.7 %all-reduce.9.cloned.1.call-start = ((), (), s32[]{:S(2)}) async-start(), calls=%async_computation.1 | async-start | bytes 8388608 | tf_op jit(solution)/shard_map/psum | solution.py:15
Sparse Core Ops, SparseCore 0:
  120.6 71.2 all-reduce.10
  195.3 150.2 all-reduce.6
  400.7 161.9 all-reduce.8
where the time goes:
time: 592 us; the launch traced here: 587 us
  waiting for transfers between devices  386 us (65%)
  other arithmetic  139 us (23%)
  local copies, waits for them, and re-layouts  31 us (5%)
  between operations  16.2 us (3%)
  matrix products  14.4 us (2%)
    psum x3, waiting for transfers between devices, spread(): return lax.psum(kept, axis)  386 us
    another operation x14, other arithmetic, body(): pivot_factor = jnp.linalg.cholesky(candidate)  78.8 us
    another operation x3, other arithmetic, right_solve(): lax.linalg.triangular_solve(payload, stacked, left_side=True, lower=True)  40.7 us
  transfers between devices with their start and end apart: 3, of which 3 were waited for; matrix products, arithmetic and copies ran while one was open for 0% of the time, Pallas kernels for 0%

commit v1 on v0

v1 whole, which is shorter than its diff:
```python
import jax
import jax.numpy as jnp
from jax import lax
from jax.experimental import pallas as pl
from jax.experimental.pallas import tpu as pltpu
from jax.sharding import PartitionSpec as P

BS = 256
N = 512
NB = 128
STEPS = N // NB
HIGHEST = lax.Precision.HIGHEST
BOTH = ("row", "col")
VMEM = pl.BlockSpec(memory_space=pltpu.VMEM)
SMEM = pl.BlockSpec(memory_space=pltpu.SMEM)


def dot_nn(a, b):
    return lax.dot_general(a, b, (((1,), (0,)), ((), ())), precision=HIGHEST, preferred_element_type=jnp.float32)


def dot_nt(a, b):
    return lax.dot_general(a, b, (((1,), (1,)), ((), ())), precision=HIGHEST, preferred_element_type=jnp.float32)


def spread_row(row):
    return jnp.broadcast_to(row, (8, NB))


def factor_block(d_ref, m_ref):
    row_ids = lax.broadcasted_iota(jnp.int32, (NB, NB), 0)
    col_ids = lax.broadcasted_iota(jnp.int32, (NB, NB), 1)
    m_ref[...] = jnp.where(row_ids == col_ids, 1.0, 0.0).astype(jnp.float32)
    for step in range(NB // 8):
        s = 8 * step
        d_rows = d_ref[s : s + 8, :]
        m_rows = m_ref[s : s + 8, :]
        cols = [spread_row(d_rows[:, s + j : s + j + 1]) for j in range(8)]
        a = {(i, j): spread_row(cols[j][i : i + 1, :]) for j in range(8) for i in range(j, 8)}
        low = {}
        inv = {}
        for j in range(8):
            r = lax.rsqrt(a[j, j])
            inv[j, j] = r
            for i in range(j + 1, 8):
                low[i, j] = a[i, j] * r
            for i in range(j + 1, 8):
                for k in range(j + 1, i + 1):
                    a[i, k] = a[i, k] - low[i, j] * low[k, j]
            for k in range(j):
                total = low[j, k] * inv[k, k]
                for t in range(k + 1, j):
                    total = total + low[j, t] * inv[t, k]
                inv[j, k] = -(r * total)

        def solve(rows):
            once = []
            for i in range(8):
                total = inv[i, 0] * rows[0]
                for k in range(1, i + 1):
                    total = total + inv[i, k] * rows[k]
                once.append(total)
            twice = []
            for k in range(8):
                total = inv[7, k] * once[7]
                for i in range(6, k - 1, -1):
                    total = total + inv[i, k] * once[i]
                twice.append(total)
            return once, twice

        _, d_twice = solve([spread_row(d_rows[k : k + 1, :]) for k in range(8)])
        m_once, m_twice = solve([spread_row(m_rows[k : k + 1, :]) for k in range(8)])
        for i in range(8):
            m_ref[s + i : s + i + 1, :] = m_once[i][0:1, :]
        for below in range(step + 1, NB // 8):
            t = 8 * below
            d_tile = d_ref[t : t + 8, :]
            d_sum = m_sum = 0.0
            for k in range(8):
                factor = spread_row(d_tile[:, s + k : s + k + 1])
                d_sum = d_sum + factor * d_twice[k]
                m_sum = m_sum + factor * m_twice[k]
            d_ref[t : t + 8, :] = d_tile - d_sum
            m_ref[t : t + 8, :] = m_ref[t : t + 8, :] - m_sum


def offset(b):
    return sum(N - NB * k for k in range(b))


def pivot_kernel(map_ref, a_ref, l_ref, inv_ref, w_ref, x_ref, d_ref, m_ref):
    coupled = map_ref[1, 0].astype(jnp.float32)
    w_ref[...] = a_ref[...]
    for b in range(2):
        start = offset(b) + BS - b * NB
        w_ref[start : offset(b + 1), :] = a_ref[start : offset(b + 1), :] * coupled
    row_ids = lax.broadcasted_iota(jnp.int32, (N, N), 0)
    col_ids = lax.broadcasted_iota(jnp.int32, (N, N), 1)
    x_ref[...] = jnp.where(row_ids == col_ids, 1.0, 0.0).astype(jnp.float32)
    for b in range(STEPS):
        o, e = b * NB, (b + 1) * NB
        panel = slice(offset(b), offset(b + 1))
        d_ref[...] = w_ref[offset(b) : offset(b) + NB, :]
        factor_block(d_ref, m_ref)
        m = m_ref[...]
        low = dot_nt(w_ref[panel, :], m)
        tri = lax.broadcasted_iota(jnp.int32, low.shape, 0) >= lax.broadcasted_iota(jnp.int32, low.shape, 1)
        l_ref[o:, o:e] = jnp.where(tri, low, 0.0)
        inv = dot_nn(m, x_ref[o:e, :e])
        inv_ref[o:e, :e] = inv
        if b:
            l_ref[:o, o:e] = jnp.zeros((o, NB), jnp.float32)
        if b < STEPS - 1:
            inv_ref[o:e, e:] = jnp.zeros((NB, N - e), jnp.float32)
            for k in range(b + 1, STEPS):
                rest = low[(k - b) * NB :]
                w_ref[offset(k) : offset(k + 1), :] -= dot_nt(rest, rest[:NB])
            x_ref[e:, :e] -= dot_nn(low[NB:], inv)


def pivot(block_map, packed):
    return pl.pallas_call(
        pivot_kernel,
        out_shape=(jax.ShapeDtypeStruct((N, N), jnp.float32),) * 2,
        in_specs=[SMEM, VMEM],
        out_specs=(VMEM, VMEM),
        scratch_shapes=[
            pltpu.VMEM((offset(STEPS), NB), jnp.float32),
            pltpu.VMEM((N, N), jnp.float32),
            pltpu.VMEM((NB, NB), jnp.float32),
            pltpu.VMEM((NB, NB), jnp.float32),
        ],
        name="pivot_cholesky",
    )(block_map, packed)


def weigh(block, w00, w01, w10, w11):
    rows = lax.broadcasted_iota(jnp.int32, block.shape, 0) < BS
    cols = lax.broadcasted_iota(jnp.int32, block.shape, 1) < BS
    return block * jnp.where(rows, jnp.where(cols, w00, w01), jnp.where(cols, w10, w11))


def update_kernel(place_ref, map_ref, front_ref, col_ref, row_ref, l_ref, inv_ref, out_ref, row_factor_ref):
    c = pl.program_id(0)
    p, q = place_ref[0], place_ref[1]
    j = c * 8 + q

    def weight(r, s):
        return map_ref[r, s].astype(jnp.float32)

    def weights(r, s):
        return [weight(2 * r + a, 2 * s + b) for a in range(2) for b in range(2)]

    @pl.when(c == 0)
    def _():
        row_factor_ref[...] = dot_nt(weigh(row_ref[...], *weights(p, 0)), inv_ref[...])

    @pl.when(p > 0)
    def _():
        @pl.when(j > 0)
        def _():
            col_factor = dot_nt(weigh(col_ref[0], *weights(j, 0)), inv_ref[...])
            front = weigh(front_ref[0], *weights(p, j))
            out_ref[0] = front - dot_nt(row_factor_ref[...], col_factor)

        @pl.when(j == 0)
        def _():
            out_ref[0] = row_factor_ref[...]

    @pl.when(p == 0)
    def _():
        @pl.when(j > 0)
        def _():
            out_ref[0] = jnp.zeros((N, N), jnp.float32)

        @pl.when(j == 0)
        def _():
            out_ref[0] = l_ref[...]


def update(place, block_map, front, cols, rows, low, inv):
    count = front.shape[0]
    tile = pl.BlockSpec((1, N, N), lambda c: (c, 0, 0))
    whole = pl.BlockSpec((N, N), lambda c: (0, 0))
    return pl.pallas_call(
        update_kernel,
        grid=(count,),
        out_shape=jax.ShapeDtypeStruct((count, N, N), jnp.float32),
        in_specs=[SMEM, SMEM, tile, tile, whole, whole, whole],
        out_specs=tile,
        scratch_shapes=[pltpu.VMEM((N, N), jnp.float32)],
        name="schur_update",
    )(place, block_map, front, cols, rows, low, inv)


def device(z, y, x, core):
    return ((z % 8 * 4 + y % 4) * 4 + x % 4) * 2 + core


def tree(value, z, y, x, core):
    rounds = [
        [([(device(0, 0, 0, 0), device(0, 0, d, 0))], x == d) for d in (1, 3, 2)],
        [([(device(0, 0, i, 0), device(0, d, i, 0)) for i in range(4)], y == d) for d in (1, 3, 2)],
        [([(device(0, j, i, 0), device(4, j, i, 0)) for j in range(4) for i in range(4)], z == 4)],
        [
            ([(device(k, j, i, 0), device(k + d, j, i, 0)) for k in (0, 4) for j in range(4) for i in range(4)], z % 4 == d % 4)
            for d in (1, 7, 2)
        ],
        [([(device(k, j, i, 0), device(k, j, i, 1)) for k in range(8) for j in range(4) for i in range(4)], core == 1)],
    ]
    for sends in rounds:
        arrived = [(hit, lax.ppermute(value, BOTH, pairs)) for pairs, hit in sends]
        for hit, got in arrived:
            value = jnp.where(hit, got, value)
    return value


def body(front_matrix, block_map):
    front = front_matrix[0, 0, :, 0]
    p = lax.axis_index("row")
    q = lax.axis_index("col")
    head = front[0]

    packed = jnp.concatenate([head[b * NB :, b * NB : (b + 1) * NB] for b in range(STEPS)], axis=0)
    packed = tree(packed, p // 4, p % 4, q // 2, q % 2)

    chunk = N // 8
    piece = jnp.zeros((chunk, N), jnp.float32)
    for t in range(8):
        pairs = [(s * 8, (s // 8 * 8 + t) * 8 + s % 8) for s in range(32)]
        got = lax.ppermute(head[t * chunk : (t + 1) * chunk], BOTH, pairs)
        piece = jnp.where(p % 8 == t, got, piece)
    cols = lax.all_gather(piece, "row").reshape(4, N, N)

    row = head
    arrived = [(x, lax.ppermute(head, "col", [(0, 2 * x)])) for x in (1, 3, 2)]
    for x, got in arrived:
        row = jnp.where(q == 2 * x, got, row)
    other = lax.ppermute(row, "col", [(2 * x, 2 * x + 1) for x in range(4)])
    row = jnp.where(q % 2 == 1, other, row)

    low, inv = pivot(block_map, packed)
    place = jnp.stack([p, q]).astype(jnp.int32)
    out = update(place, block_map, front, cols, row, low, inv)
    return out.reshape(front_matrix.shape)


def solution(mesh):
    return jax.shard_map(
        body,
        mesh=mesh,
        in_specs=(P(None, "row", None, "col", None, None), P()),
        out_specs=P(None, "row", None, "col", None, None),
        check_vma=False,
    )
```

time: 592 us -> 175 us (0.30)
  the two profiles are of different devices: /device:TPU:10 before, /device:TPU:213 now
where the time goes in v1:
time: 175 us; the launch traced here: 174 us
  waiting for transfers between devices  75.2 us (43%)
  Pallas kernels  46.6 us (27%)
  starting transfers between devices  25.5 us (15%)
  between operations  13.7 us (8%)
  other arithmetic  8.94 us (5%)
  local copies, waits for them, and re-layouts  4.4 us (3%)
    ppermute x11, waiting for transfers between devices, tree(): arrived = [(hit, lax.ppermute(value, BOTH, pairs)) for pairs, hit in sends]  48.8 us
    pallas_call x1, Pallas kernels, pivot(): pl.pallas_call(pivot_kernel, out_shape=(jax.ShapeDtypeStruct((N, N), jnp....  26.4 us
    ppermute x1, waiting for transfers between devices, body(): other = lax.ppermute(row, 'col', [(2 * x, 2 * x + 1) for x in range(4)])  20.5 us
    pallas_call x1, Pallas kernels, update(): pl.pallas_call(update_kernel, grid=(count,), out_shape=jax.ShapeDtypeStru...  20.3 us
    ppermute x11, starting transfers between devices, tree(): arrived = [(hit, lax.ppermute(value, BOTH, pairs)) for pairs, hit in sends]  14.2 us
    ppermute x8, starting transfers between devices, body(): got = lax.ppermute(head[t * chunk:(t + 1) * chunk], BOTH, pairs)  5.96 us
    ppermute x8, waiting for transfers between devices, body(): got = lax.ppermute(head[t * chunk:(t + 1) * chunk], BOTH, pairs)  5.91 us
    select_n x5, other arithmetic, tree(): value = jnp.where(hit, got, value)  4.6 us
  transfers between devices with their start and end apart: 24, of which 3 were waited for; matrix products, arithmetic and copies ran while one was open for 5% of the time, Pallas kernels for 15%

profile of v1, /device:TPU:213, one launch (start us, length us, event | category | flops | bytes accessed | tf_op | source)
XLA Modules:
  0.0 174.4 jit_solution(15862077449505675710)
XLA Ops:
  6.5 0.0 all-gather.3.cloned.1.call-start
  6.5 1.4 slice_bitcast_fusion.1
  7.9 0.7 collective-permute-start.7
  8.6 0.7 collective-permute-start.6
  9.3 1.3 collective-permute-start.5
  10.6 0.7 collective-permute-start.4
  11.2 0.7 collective-permute-start.3
  11.9 0.0 collective-permute-done.7
  11.9 0.7 collective-permute-start.2
  12.6 0.0 collective-permute-done.6
  12.6 0.7 collective-permute-start.1
  13.3 5.9 %collective-permute-done.5 = f32[64,512]{1,0:T(8,128)S(1)} collective-permute-done((f32[64,512]{1,0:T(8,128)S(1)}, f32[64,512]{1,0:T(8,128)S(1)}, u32[]{:S(2)}, u32[]{:S(2)}) %collective-permute-start.5) | collective-permute-done | bytes 131104 | tf_op jit(solution)/shard_map/ppermute | solution.py:231
  19.2 0.7 collective-permute-start
  19.9 0.0 collective-permute-done.4
  19.9 0.0 collective-permute-done.3
  19.9 0.0 collective-permute-done.2
  19.9 0.0 collective-permute-done.1
  19.9 0.0 collective-permute-done
  19.9 0.7 select_select_fusion.4
  20.7 0.0 all-gather.3.cloned.1.call-update
  20.7 1.3 slice_bitcast_fusion
  22.2 0.7 collective-permute-start.14
  22.9 1.5 collective-permute-start.13
  24.4 1.5 collective-permute-start.12
  25.9 0.0 collective-permute-done.14
  25.9 0.0 collective-permute-done.13
  25.9 0.0 collective-permute-done.12
  25.9 1.2 select_select_fusion.3
  27.2 1.5 collective-permute-start.17
  28.7 0.7 collective-permute-start.16
  29.4 1.5 collective-permute-start.15
  30.9 0.0 collective-permute-done.17
  30.9 0.0 collective-permute-done.16
  30.9 0.8 copy-done.1
  31.8 0.0 collective-permute-done.15
  31.8 1.2 select_select_fusion.2
  33.0 1.5 collective-permute-start.18
  34.5 0.7 collective-permute-start.10
  35.2 1.7 collective-permute-start.9
  36.9 1.7 collective-permute-start.8
  38.5 0.0 collective-permute-done.18
  38.5 0.1 broadcast_select_fusion.1
  38.6 0.7 collective-permute-start.21
  39.3 1.5 collective-permute-start.20
  40.8 0.0 collective-permute-done.10
  40.8 1.5 collective-permute-start.19
  42.3 0.0 collective-permute-done.9
  42.3 0.0 collective-permute-done.8
  42.3 1.7 select_select_fusion
  44.1 1.3 collective-permute-start.11
  45.4 0.0 collective-permute-done.21
  45.4 0.0 copy-start
  45.4 0.0 collective-permute-done.20
  45.4 0.8 copy-done
  46.2 0.0 collective-permute-done.19
  46.2 1.2 select_select_fusion.1
  47.5 1.5 collective-permute-start.22
  48.9 0.6 pad_add_fusion.place_ref
  49.6 20.5 %collective-permute-done.11 = f32[512,512]{1,0:T(8,128)S(1)} collective-permute-done((f32[512,512]{1,0:T(8,128)S(1)}, f32[512,512]{1,0:T(8,128)S(1)}, u32[]{:S(2)}, u32[]{:S(2)}) %collective-permute-start.11) | collective-permute-done | bytes 1048608 | tf_op jit(solution)/shard_map/ppermute | solution.py:239
  70.1 1.2 broadcast_select_fusion.row_ref
  71.3 48.7 %collective-permute-done.22 = f32[1280,128]{1,0:T(8,128)S(1)} collective-permute-done((f32[1280,128]{1,0:T(8,128)S(1)}, f32[1280,128]{1,0:T(8,128)S(1)}, u32[]{:S(2)}, u32[]{:S(2)}) %collective-permute-start.22) | collective-permute-done | bytes 655392 | tf_op jit(solution)/shard_map/ppermute | solution.py:212
  120.0 0.9 broadcast_select_fusion.2.a_ref
  120.9 26.4 %pivot_cholesky.1 = (f32[512,512]{1,0:T(8,128)}, f32[512,512]{1,0:T(8,128)}) custom-call(s32[64,64]{1,0:T(8,128)} %map_ref.3, f32[1280,128]{1,0:T(8,128)} %broadcast_select_fusion.2.a_ref), custom_call_target="tpu_custom_call" | custom-call | tf_op jit(solution)/shard_map/pivot_cholesky/pallas_call | solution.py:122
  147.3 20.3 %schur_update.1 = f32[4,512,512]{2,1,0:T(8,128)} custom-call(s32[2]{0:T(128)} %pad_add_fusion.place_ref, s32[64,64]{1,0:T(8,128)} %map_ref.3, f32[4,512,512]{2,1,0:T(8,128)} %bitcast.27, f32[4,512,512]{2,1,0:T(8,128)} %bitcast.28, f32[512,512]{1,0:T(8,128)} %broadcast_select_fusion.row_ref, f32[512,512]{1,0:T(8,128)} %get-tuple-element.7.l_ref, ...), custom_call_target="tpu_custom_call" | custom-call | tf_op jit(solution)/shard_map/schur_update/pallas_call | solution.py:185
  (7 shorter events, 0.1 us)
Async XLA Ops:
  6.5 140.8 %all-gather.3.cloned.1.call-start = ((), (), s32[]{:S(2)}) async-start(), calls=%async_computation | async-start | bytes 4325376 | tf_op jit(solution)/shard_map/all_gather | solution.py:233
  7.9 4.0 %collective-permute-start.7 = (f32[64,512]{1,0:T(8,128)S(1)}, f32[64,512]{1,0:T(8,128)S(1)}, u32[]{:S(2)}, u32[]{:S(2)}) collective-permute-start(f32[64,512]{1,0:T(8,128)S(1)} %get-tuple-element.9), channel_id=1, source_target_pairs={{0,0},{8,1},{16,2},{24,3},{32,4},{40,5},{48,6},{56,7},{64,64},{72,... | collective-permute-start | bytes 393224 | tf_op jit(solution)/shard_map/ppermute | solution.py:231
  8.6 4.0 %collective-permute-start.6 = (f32[64,512]{1,0:T(8,128)S(1)}, f32[64,512]{1,0:T(8,128)S(1)}, u32[]{:S(2)}, u32[]{:S(2)}) collective-permute-start(f32[64,512]{1,0:T(8,128)S(1)} %get-tuple-element.10), channel_id=1, source_target_pairs={{0,8},{8,9},{16,10},{24,11},{32,12},{40,13},{48,14},{56,15},{64,72... | collective-permute-start | bytes 393224 | tf_op jit(solution)/shard_map/ppermute | solution.py:231
  9.3 9.9 %collective-permute-start.5 = (f32[64,512]{1,0:T(8,128)S(1)}, f32[64,512]{1,0:T(8,128)S(1)}, u32[]{:S(2)}, u32[]{:S(2)}) collective-permute-start(f32[64,512]{1,0:T(8,128)S(1)} %get-tuple-element.11), channel_id=1, source_target_pairs={{0,16},{8,17},{16,18},{24,19},{32,20},{40,21},{48,22},{56,23},{64,... | collective-permute-start | bytes 393224 | tf_op jit(solution)/shard_map/ppermute | solution.py:231
  10.6 9.3 %collective-permute-start.4 = (f32[64,512]{1,0:T(8,128)S(1)}, f32[64,512]{1,0:T(8,128)S(1)}, u32[]{:S(2)}, u32[]{:S(2)}) collective-permute-start(f32[64,512]{1,0:T(8,128)S(1)} %get-tuple-element.12), channel_id=1, source_target_pairs={{0,24},{8,25},{16,26},{24,27},{32,28},{40,29},{48,30},{56,31},{64,... | collective-permute-start | bytes 393224 | tf_op jit(solution)/shard_map/ppermute | solution.py:231
  11.2 8.6 %collective-permute-start.3 = (f32[64,512]{1,0:T(8,128)S(1)}, f32[64,512]{1,0:T(8,128)S(1)}, u32[]{:S(2)}, u32[]{:S(2)}) collective-permute-start(f32[64,512]{1,0:T(8,128)S(1)} %get-tuple-element.13), channel_id=1, source_target_pairs={{0,32},{8,33},{16,34},{24,35},{32,36},{40,37},{48,38},{56,39},{64,... | collective-permute-start | bytes 393224 | tf_op jit(solution)/shard_map/ppermute | solution.py:231
  11.9 8.0 %collective-permute-start.2 = (f32[64,512]{1,0:T(8,128)S(1)}, f32[64,512]{1,0:T(8,128)S(1)}, u32[]{:S(2)}, u32[]{:S(2)}) collective-permute-start(f32[64,512]{1,0:T(8,128)S(1)} %get-tuple-element.14), channel_id=1, source_target_pairs={{0,40},{8,41},{16,42},{24,43},{32,44},{40,45},{48,46},{56,47},{64,... | collective-permute-start | bytes 393224 | tf_op jit(solution)/shard_map/ppermute | solution.py:231
  12.6 7.3 %collective-permute-start.1 = (f32[64,512]{1,0:T(8,128)S(1)}, f32[64,512]{1,0:T(8,128)S(1)}, u32[]{:S(2)}, u32[]{:S(2)}) collective-permute-start(f32[64,512]{1,0:T(8,128)S(1)} %get-tuple-element.15), channel_id=1, source_target_pairs={{0,48},{8,49},{16,50},{24,51},{32,52},{40,53},{48,54},{56,55},{64,... | collective-permute-start | bytes 393224 | tf_op jit(solution)/shard_map/ppermute | solution.py:231
  19.2 0.7 collective-permute-start
  22.2 3.8 %collective-permute-start.14 = (f32[1280,128]{1,0:T(8,128)S(1)}, f32[1280,128]{1,0:T(8,128)S(1)}, u32[]{:S(2)}, u32[]{:S(2)}) collective-permute-start(f32[1280,128]{1,0:T(8,128)S(1)} %pad_maximum_fusion), channel_id=1, source_target_pairs={{0,2}} | collective-permute-start | bytes 1966088 | tf_op jit(solution)/shard_map/ppermute | solution.py:212
  22.9 3.1 %collective-permute-start.13 = (f32[1280,128]{1,0:T(8,128)S(1)}, f32[1280,128]{1,0:T(8,128)}, u32[]{:S(2)}, u32[]{:S(2)}) collective-permute-start(f32[1280,128]{1,0:T(8,128)S(1)} %pad_maximum_fusion), channel_id=1, source_target_pairs={{0,6}} | collective-permute-start | bytes 1966088 | tf_op jit(solution)/shard_map/ppermute | solution.py:212
  24.4 1.5 collective-permute-start.12
  27.2 3.8 %collective-permute-start.17 = (f32[1280,128]{1,0:T(8,128)S(1)}, f32[1280,128]{1,0:T(8,128)}, u32[]{:S(2)}, u32[]{:S(2)}) collective-permute-start(f32[1280,128]{1,0:T(8,128)S(1)} %select_select_fusion.3), channel_id=1, source_target_pairs={{0,8},{2,10},{4,12},{6,14}} | collective-permute-start | bytes 1966088 | tf_op jit(solution)/shard_map/ppermute | solution.py:212
  28.7 2.2 %collective-permute-start.16 = (f32[1280,128]{1,0:T(8,128)S(1)}, f32[1280,128]{1,0:T(8,128)S(1)}, u32[]{:S(2)}, u32[]{:S(2)}) collective-permute-start(f32[1280,128]{1,0:T(8,128)S(1)} %select_select_fusion.3), channel_id=1, source_target_pairs={{0,24},{2,26},{4,28},{6,30}} | collective-permute-start | bytes 1966088 | tf_op jit(solution)/shard_map/ppermute | solution.py:212
  29.4 2.4 %collective-permute-start.15 = (f32[1280,128]{1,0:T(8,128)S(1)}, f32[1280,128]{1,0:T(8,128)}, u32[]{:S(2)}, u32[]{:S(2)}) collective-permute-start(f32[1280,128]{1,0:T(8,128)S(1)} %select_select_fusion.3), channel_id=1, source_target_pairs={{0,16},{2,18},{4,20},{6,22}} | collective-permute-start | bytes 1966088 | tf_op jit(solution)/shard_map/ppermute | solution.py:212
  30.9 0.8 copy-start.1
  33.0 5.6 %collective-permute-start.18 = (f32[1280,128]{1,0:T(8,128)S(1)}, f32[1280,128]{1,0:T(8,128)}, u32[]{:S(2)}, u32[]{:S(2)}) collective-permute-start(f32[1280,128]{1,0:T(8,128)S(1)} %select_select_fusion.2), channel_id=1, source_target_pairs={{0,128},{2,130},{4,132},{6,134},{8,136},{10,138},{12,140},{14,142}... | collective-permute-start | bytes 1966088 | tf_op jit(solution)/shard_map/ppermute | solution.py:212
  34.5 6.3 %collective-permute-start.10 = (f32[512,512]{1,0:T(8,128)S(1)}, f32[512,512]{1,0:T(8,128)S(1)}, u32[]{:S(2)}, u32[]{:S(2)}) collective-permute-start(f32[512,512]{1,0:T(8,128)S(1)} %slice_bitcast_fusion), channel_id=1, source_target_pairs={{0,2},{8,10},{16,18},{24,26},{32,34},{40,42},{48,50},{56,58},{64,6... | collective-permute-start | bytes 3145736 | tf_op jit(solution)/shard_map/ppermute | solution.py:236
  35.2 7.1 %collective-permute-start.9 = (f32[512,512]{1,0:T(8,128)S(1)}, f32[512,512]{1,0:T(8,128)}, u32[]{:S(2)}, u32[]{:S(2)}) collective-permute-start(f32[512,512]{1,0:T(8,128)S(1)} %slice_bitcast_fusion), channel_id=1, source_target_pairs={{0,6},{8,14},{16,22},{24,30},{32,38},{40,46},{48,54},{56,62},{64,7... | collective-permute-start | bytes 3145736 | tf_op jit(solution)/shard_map/ppermute | solution.py:236
  36.9 5.5 %collective-permute-start.8 = (f32[512,512]{1,0:T(8,128)S(1)}, f32[512,512]{1,0:T(8,128)}, u32[]{:S(2)}, u32[]{:S(2)}) collective-permute-start(f32[512,512]{1,0:T(8,128)S(1)} %slice_bitcast_fusion), channel_id=1, source_target_pairs={{0,4},{8,12},{16,20},{24,28},{32,36},{40,44},{48,52},{56,60},{64,6... | collective-permute-start | bytes 3145736 | tf_op jit(solution)/shard_map/ppermute | solution.py:236
  38.6 6.8 %collective-permute-start.21 = (f32[1280,128]{1,0:T(8,128)S(1)}, f32[1280,128]{1,0:T(8,128)S(1)}, u32[]{:S(2)}, u32[]{:S(2)}) collective-permute-start(f32[1280,128]{1,0:T(8,128)S(1)} %broadcast_select_fusion.1), channel_id=1, source_target_pairs={{0,32},{2,34},{4,36},{6,38},{8,40},{10,42},{12,44},{14,46},{16,48}... | collective-permute-start | bytes 1966088 | tf_op jit(solution)/shard_map/ppermute | solution.py:212
  39.3 6.1 %collective-permute-start.20 = (f32[1280,128]{1,0:T(8,128)S(1)}, f32[1280,128]{1,0:T(8,128)}, u32[]{:S(2)}, u32[]{:S(2)}) collective-permute-start(f32[1280,128]{1,0:T(8,128)S(1)} %broadcast_select_fusion.1), channel_id=1, source_target_pairs={{0,224},{2,226},{4,228},{6,230},{8,232},{10,234},{12,236},{14,238}... | collective-permute-start | bytes 1966088 | tf_op jit(solution)/shard_map/ppermute | solution.py:212
  40.8 5.4 %collective-permute-start.19 = (f32[1280,128]{1,0:T(8,128)S(1)}, f32[1280,128]{1,0:T(8,128)}, u32[]{:S(2)}, u32[]{:S(2)}) collective-permute-start(f32[1280,128]{1,0:T(8,128)S(1)} %broadcast_select_fusion.1), channel_id=1, source_target_pairs={{0,64},{2,66},{4,68},{6,70},{8,72},{10,74},{12,76},{14,78},{16,80}... | collective-permute-start | bytes 1966088 | tf_op jit(solution)/shard_map/ppermute | solution.py:212
  44.1 26.0 %collective-permute-start.11 = (f32[512,512]{1,0:T(8,128)S(1)}, f32[512,512]{1,0:T(8,128)S(1)}, u32[]{:S(2)}, u32[]{:S(2)}) collective-permute-start(f32[512,512]{1,0:T(8,128)S(1)} %select_select_fusion), channel_id=1, source_target_pairs={{0,1},{2,3},{4,5},{6,7},{8,9},{10,11},{12,13},{14,15},{16,17},{18,... | collective-permute-start | bytes 3145736 | tf_op jit(solution)/shard_map/ppermute | solution.py:239
  45.4 0.8 copy-start
  47.5 72.6 %collective-permute-start.22 = (f32[1280,128]{1,0:T(8,128)S(1)}, f32[1280,128]{1,0:T(8,128)S(1)}, u32[]{:S(2)}, u32[]{:S(2)}) collective-permute-start(f32[1280,128]{1,0:T(8,128)S(1)} %select_select_fusion.1), channel_id=1, source_target_pairs={{0,1},{2,3},{4,5},{6,7},{8,9},{10,11},{12,13},{14,15},{16,17},{18,... | collective-permute-start | bytes 1966088 | tf_op jit(solution)/shard_map/ppermute | solution.py:212
Sparse Core Ops, SparseCore 0:
  20.8 88.6 all-gather.2

commit v2 on v1

--- a/solution.py
+++ b/solution.py
@@ -9,6 +9,7 @@
 N = 512
 NB = 128
 STEPS = N // NB
+SPLIT = 16
 HIGHEST = lax.Precision.HIGHEST
 BOTH = ("row", "col")
 VMEM = pl.BlockSpec(memory_space=pltpu.VMEM)
@@ -140,7 +141,7 @@
     return block * jnp.where(rows, jnp.where(cols, w00, w01), jnp.where(cols, w10, w11))
 
 
-def update_kernel(place_ref, map_ref, front_ref, col_ref, row_ref, l_ref, inv_ref, out_ref, row_factor_ref):
+def update_kernel(place_ref, map_ref, front_ref, upper_ref, lower_ref, row_ref, l_ref, inv_ref, out_ref, row_factor_ref, col_ref):
     c = pl.program_id(0)
     p, q = place_ref[0], place_ref[1]
     j = c * 8 + q
@@ -159,7 +160,11 @@
     def _():
         @pl.when(j > 0)
         def _():
-            col_factor = dot_nt(weigh(col_ref[0], *weights(j, 0)), inv_ref[...])
+            for t in range(8):
+                start = t * (N // 8)
+                col_ref[start : start + SPLIT, :] = upper_ref[0, t // 4, t % 4]
+                col_ref[start + SPLIT : start + N // 8, :] = lower_ref[t % 4, 0, t // 4]
+            col_factor = dot_nt(weigh(col_ref[...], *weights(j, 0)), inv_ref[...])
             front = weigh(front_ref[0], *weights(p, j))
             out_ref[0] = front - dot_nt(row_factor_ref[...], col_factor)
 
@@ -178,7 +183,7 @@
             out_ref[0] = l_ref[...]
 
 
-def update(place, block_map, front, cols, rows, low, inv):
+def update(place, block_map, front, upper, lower, rows, low, inv):
     count = front.shape[0]
     tile = pl.BlockSpec((1, N, N), lambda c: (c, 0, 0))
     whole = pl.BlockSpec((N, N), lambda c: (0, 0))
@@ -186,27 +191,43 @@
         update_kernel,
         grid=(count,),
         out_shape=jax.ShapeDtypeStruct((count, N, N), jnp.float32),
-        in_specs=[SMEM, SMEM, tile, tile, whole, whole, whole],
+        in_specs=[
+            SMEM,
+            SMEM,
+            tile,
+            pl.BlockSpec((1, 2, 4, SPLIT, N), lambda c: (c, 0, 0, 0, 0)),
+            pl.BlockSpec((4, 1, 2, N // 8 - SPLIT, N), lambda c: (0, c, 0, 0, 0)),
+            whole,
+            whole,
+            whole,
+        ],
         out_specs=tile,
-        scratch_shapes=[pltpu.VMEM((N, N), jnp.float32)],
+        scratch_shapes=[pltpu.VMEM((N, N), jnp.float32), pltpu.VMEM((N, N), jnp.float32)],
         name="schur_update",
-    )(place, block_map, front, cols, rows, low, inv)
+    )(place, block_map, front, upper, lower, rows, low, inv)
 
 
 def device(z, y, x, core):
     return ((z % 8 * 4 + y % 4) * 4 + x % 4) * 2 + core
 
 
-def tree(value, z, y, x, core):
+Y_GROUPS = [[z * 4 + y for y in range(4)] for z in range(8)]
+Z_GROUPS = [[z * 4 + y for z in range(8)] for y in range(4)]
+
+
+def gather(value, axis, size, groups=None):
+    return lax.all_to_all(jnp.broadcast_to(value, (size, *value.shape)), axis, 0, 0, axis_index_groups=groups)
+
+
+def plane_tree(value, z, y):
+    lanes = [(i, k) for i in range(4) for k in range(2)]
     rounds = [
-        [([(device(0, 0, 0, 0), device(0, 0, d, 0))], x == d) for d in (1, 3, 2)],
-        [([(device(0, 0, i, 0), device(0, d, i, 0)) for i in range(4)], y == d) for d in (1, 3, 2)],
-        [([(device(0, j, i, 0), device(4, j, i, 0)) for j in range(4) for i in range(4)], z == 4)],
+        [([(device(0, 0, i, k), device(0, d, i, k)) for i, k in lanes], y == d) for d in (1, 3, 2)],
+        [([(device(0, j, i, k), device(4, j, i, k)) for j in range(4) for i, k in lanes], z == 4)],
         [
-            ([(device(k, j, i, 0), device(k + d, j, i, 0)) for k in (0, 4) for j in range(4) for i in range(4)], z % 4 == d % 4)
+            ([(device(s, j, i, k), device(s + d, j, i, k)) for s in (0, 4) for j in range(4) for i, k in lanes], z % 4 == d % 4)
             for d in (1, 7, 2)
         ],
-        [([(device(k, j, i, 0), device(k, j, i, 1)) for k in range(8) for j in range(4) for i in range(4)], core == 1)],
     ]
     for sends in rounds:
         arrived = [(hit, lax.ppermute(value, BOTH, pairs)) for pairs, hit in sends]
@@ -222,7 +243,9 @@
     head = front[0]
 
     packed = jnp.concatenate([head[b * NB :, b * NB : (b + 1) * NB] for b in range(STEPS)], axis=0)
-    packed = tree(packed, p // 4, p % 4, q // 2, q % 2)
+    share = lax.all_to_all(packed.reshape(8, -1, NB), "col", 0, 0)[0]
+    share = plane_tree(share, p // 4, p % 4)
+    packed = gather(share, "col", 8).reshape(-1, NB)
 
     chunk = N // 8
     piece = jnp.zeros((chunk, N), jnp.float32)
@@ -230,7 +253,11 @@
         pairs = [(s * 8, (s // 8 * 8 + t) * 8 + s % 8) for s in range(32)]
         got = lax.ppermute(head[t * chunk : (t + 1) * chunk], BOTH, pairs)
         piece = jnp.where(p % 8 == t, got, piece)
-    cols = lax.all_gather(piece, "row").reshape(4, N, N)
+    upper, lower = piece[:SPLIT], piece[SPLIT:]
+    lower = gather(lower, "row", 8, Z_GROUPS)
+    upper = gather(upper, "row", 4, Y_GROUPS)
+    lower = gather(lower, "row", 4, Y_GROUPS).reshape(4, 4, 2, chunk - SPLIT, N)
+    upper = gather(upper, "row", 8, Z_GROUPS).reshape(4, 2, 4, SPLIT, N)
 
     row = head
     arrived = [(x, lax.ppermute(head, "col", [(0, 2 * x)])) for x in (1, 3, 2)]
@@ -241,7 +268,7 @@
 
     low, inv = pivot(block_map, packed)
     place = jnp.stack([p, q]).astype(jnp.int32)
-    out = update(place, block_map, front, cols, row, low, inv)
+    out = update(place, block_map, front, upper, lower, row, low, inv)
     return out.reshape(front_matrix.shape)
 
 

time: 175 us -> 202 us (1.15)
  the two profiles are of different devices: /device:TPU:213 before, /device:TPU:10 now
where the time goes in v2:
time: 202 us; the launch traced here: 201 us
  starting transfers between devices  52.9 us (26%)
  Pallas kernels  46.7 us (23%)
  blocking collectives  41.6 us (21%)
  waiting for transfers between devices  39.1 us (19%)
  local copies, waits for them, and re-layouts  13.8 us (7%)
  other arithmetic  6.36 us (3%)
    all_to_all x4, waiting for transfers between devices, gather(): lax.all_to_all(jnp.broadcast_to(value, (size, *value.shape)), axis, 0, 0,...  37.1 us
    all_to_all x1, blocking collectives, gather(): lax.all_to_all(jnp.broadcast_to(value, (size, *value.shape)), axis, 0, 0,...  26.7 us
    pallas_call x1, Pallas kernels, pivot(): pl.pallas_call(pivot_kernel, out_shape=(jax.ShapeDtypeStruct((N, N), jnp....  26.4 us
    all_to_all x4, starting transfers between devices, gather(): lax.all_to_all(jnp.broadcast_to(value, (size, *value.shape)), axis, 0, 0,...  25.4 us
    pallas_call x1, Pallas kernels, update(): pl.pallas_call(update_kernel, grid=(count,), out_shape=jax.ShapeDtypeStru...  20.3 us
    all_to_all x1, blocking collectives, body(): share = lax.all_to_all(packed.reshape(8, -1, NB), 'col', 0, 0)[0]  15 us
    ppermute x7, starting transfers between devices, plane_tree(): arrived = [(hit, lax.ppermute(value, BOTH, pairs)) for pairs, hit in sends]  14.7 us
    ppermute x8, starting transfers between devices, body(): got = lax.ppermute(head[t * chunk:(t + 1) * chunk], BOTH, pairs)  5.95 us
  transfers between devices with their start and end apart: 23, of which 5 were waited for; matrix products, arithmetic and copies ran while one was open for 5% of the time, Pallas kernels for 13%

profile of v2, /device:TPU:10, one launch (start us, length us, event | category | flops | bytes accessed | tf_op | source)
XLA Modules:
  0.0 200.9 jit_solution(9231552469231747113)
XLA Ops:
  0.0 2.3 %slice_bitcast_fusion = f32[512,512]{1,0:T(8,128)} fusion(f32[1,1,4,1,512,512]{5,4,3,2,1,0:T(8,128)} %param.2), kind=kLoop, calls=%fused_computation.1 | loop fusion | bytes 2097152 | tf_op jit(solution)/shard_map/squeeze | solution.py:243
  2.3 0.8 slice.110
  3.1 0.9 slice.109
  4.0 0.9 slice.108
  5.0 1.0 slice.107
  6.0 15.0 %all_to_all.30 = f32[8,160,128]{2,1,0:T(8,128)S(1)} all-to-all(f32[8,160,128]{2,1,0:T(8,128)S(1)} %bitcast.38), channel_id=1, replica_groups=mesh['row'=32,'col'=8] {'col'}, dimensions={0} | all-to-all | bytes 1310720 | tf_op jit(solution)/shard_map/all_to_all | solution.py:246
  21.0 1.3 collective-permute-start.14
  22.3 0.7 collective-permute-start.13
  22.9 0.7 collective-permute-start.12
  23.6 1.4 slice_bitcast_fusion.1
  25.0 0.7 collective-permute-start.7
  25.7 1.3 collective-permute-start.6
  27.0 0.3 collective-permute-done.14
  27.3 0.7 collective-permute-start.5
  28.0 0.0 collective-permute-done.13
  28.0 0.0 collective-permute-done.12
  28.0 8.2 %collective-permute-start.15 = (f32[160,128]{1,0:T(8,128)S(1)}, f32[160,128]{1,0:T(8,128)S(1)}, u32[]{:S(2)}, u32[]{:S(2)}) collective-permute-start(f32[160,128]{1,0:T(8,128)S(1)} %select_select_fusion.3), channel_id=1, source_target_pairs={{0,128},{1,129},{2,130},{3,131},{4,132},{5,133},{6,134},{7,135},{8... | collective-permute-start | bytes 245768 | tf_op jit(solution)/shard_map/ppermute | solution.py:233
  36.2 0.7 collective-permute-start.4
  37.0 0.0 collective-permute-done.7
  37.0 0.7 collective-permute-start.3
  37.7 1.7 collective-permute-done.6
  39.3 0.7 collective-permute-start.2
  40.0 0.0 collective-permute-done.5
  40.0 0.7 collective-permute-start.1
  40.7 0.0 collective-permute-done.15
  40.7 0.7 collective-permute-start
  41.4 0.0 collective-permute-done.4
  41.4 1.3 collective-permute-start.18
  42.7 0.0 collective-permute-done.3
  42.7 1.3 collective-permute-start.17
  44.0 0.0 collective-permute-done.2
  44.0 1.3 collective-permute-start.16
  45.3 0.0 collective-permute-done.1
  45.3 0.0 collective-permute-done
  45.3 0.1 select_select_fusion.1
  45.4 0.7 broadcast_in_dim.19
  46.1 9.0 %all-to-all-start = ((f32[4,16,512]{2,1,0:T(8,128)}), f32[4,16,512]{2,1,0:T(8,128)S(1)}, u32[]{:S(2)}, u32[]{:S(2)}) async-start(f32[4,16,512]{2,1,0:T(8,128)} %broadcast_in_dim.19), calls=%async_computation | async-start | bytes 262144 | tf_op jit(solution)/shard_map/all_to_all | solution.py:219
  55.1 0.0 collective-permute-done.18
  55.1 0.0 collective-permute-done.17
  55.1 0.0 collective-permute-done.16
  55.2 4.5 %all-to-all-done = f32[4,16,512]{2,1,0:T(8,128)S(1)} async-done(((f32[4,16,512]{2,1,0:T(8,128)}), f32[4,16,512]{2,1,0:T(8,128)S(1)}, u32[]{:S(2)}, u32[]{:S(2)}) %all-to-all-start) | async-done | bytes 131104 | tf_op jit(solution)/shard_map/all_to_all | solution.py:219
  59.7 0.9 broadcast_in_dim.23
  60.5 7.7 %all-to-all-start.5 = ((f32[8,160,128]{2,1,0:T(8,128)}), f32[8,160,128]{2,1,0:T(8,128)S(1)}, u32[]{:S(2)}, u32[]{:S(2)}) async-start(f32[8,160,128]{2,1,0:T(8,128)} %broadcast_in_dim.23), calls=%async_computation.5 | async-start | bytes 1310720 | tf_op jit(solution)/shard_map/all_to_all | solution.py:219
  68.3 10.3 %all-to-all-done.5 = f32[8,160,128]{2,1,0:T(8,128)S(1)} async-done(((f32[8,160,128]{2,1,0:T(8,128)}), f32[8,160,128]{2,1,0:T(8,128)S(1)}, u32[]{:S(2)}, u32[]{:S(2)}) %all-to-all-start.5) | async-done | bytes 655392 | tf_op jit(solution)/shard_map/all_to_all | solution.py:219
  78.6 0.1 broadcast_in_dim.21
  78.7 26.7 %all_to_all.31 = f32[8,48,512]{2,1,0:T(8,128)S(1)} all-to-all(f32[8,48,512]{2,1,0:T(8,128)S(1)} %broadcast_in_dim.21), channel_id=1, replica_groups={{0,32,64,96,128,160,192,224},{8,40,72,104,136,168,200,232},{16,48,80,11..., dimensions={0} | all-to-all | bytes 1572864 | tf_op jit(solution)/shard_map/all_to_all | solution.py:219
  105.3 1.1 broadcast_in_dim.20
  106.4 3.6 %all-to-all-start.1 = ((f32[8,4,16,512]{3,2,1,0:T(8,128)}), f32[8,4,16,512]{3,2,1,0:T(8,128)S(1)}, u32[]{:S(2)}, u32[]{:S(2)}) async-start(f32[8,4,16,512]{3,2,1,0:T(8,128)} %broadcast_in_dim.20), calls=%async_computation.1 | async-start | bytes 2097152 | tf_op jit(solution)/shard_map/all_to_all | solution.py:219
  110.0 1.3 collective-permute-start.10
  111.3 1.7 collective-permute-start.9
  113.0 1.6 collective-permute-start.8
  114.6 22.3 %all-to-all-done.1 = f32[8,4,16,512]{3,2,1,0:T(8,128)S(1)} async-done(((f32[8,4,16,512]{3,2,1,0:T(8,128)}), f32[8,4,16,512]{3,2,1,0:T(8,128)S(1)}, u32[]{:S(2)}, u32[]{:S(2)}) %all-to-all-start.1) | async-done | bytes 1048608 | tf_op jit(solution)/shard_map/all_to_all | solution.py:219
  136.9 2.1 %broadcast_in_dim.22 = f32[4,8,48,512]{3,2,1,0:T(8,128)} broadcast(f32[8,48,512]{2,1,0:T(8,128)S(1)} %all_to_all.31), dimensions={1,2,3} | broadcast | bytes 3932160 | tf_op jit(solution)/shard_map/broadcast_in_dim | solution.py:219
  139.0 5.1 %all-to-all-start.3 = ((f32[4,8,48,512]{3,2,1,0:T(8,128)}), f32[4,8,48,512]{3,2,1,0:T(8,128)S(1)}, u32[]{:S(2)}, u32[]{:S(2)}) async-start(f32[4,8,48,512]{3,2,1,0:T(8,128)} %broadcast_in_dim.22), calls=%async_computation.3 | async-start | bytes 6291456 | tf_op jit(solution)/shard_map/all_to_all | solution.py:219
  144.1 0.0 collective-permute-done.10
  144.1 3.1 %select_select_fusion = f32[512,512]{1,0:T(8,128)} fusion(f32[512,512]{1,0:T(8,128)} %collective-permute-done.8, f32[512,512]{1,0:T(8,128)} %collective-permute-done.9, f32[512,512]{1,0:T(8,128)} %collective-permute-done.10, pred[]{:T(512)S(6)} %eq.82, pred[]{:T(512)S(6)} %eq.81, pred[]{:T(512)S(6)} %eq.80, f32[1,1,4,1,512,512]{5,4,3,2,1,0:T(8,128)} %param.2), kind=kLoop, calls=%fused_computation | loop fusion | flops 786432 | bytes 5242883 | tf_op jit(solution)/shard_map/jit(_where)/select_n | solution.py:265
  147.2 2.3 %collective-permute-start.11 = (f32[512,512]{1,0:T(8,128)}, f32[512,512]{1,0:T(8,128)}, u32[]{:S(2)}, u32[]{:S(2)}) collective-permute-start(f32[512,512]{1,0:T(8,128)} %select_select_fusion), channel_id=1, source_target_pairs={{0,1},{2,3},{4,5},{6,7},{8,9},{10,11},{12,13},{14,15},{16,17},{18,... | collective-permute-start | bytes 3145736 | tf_op jit(solution)/shard_map/ppermute | solution.py:266
  149.4 0.6 pad_add_fusion.place_ref
  150.1 26.4 %pivot_cholesky.1 = (f32[512,512]{1,0:T(8,128)}, f32[512,512]{1,0:T(8,128)}) custom-call(s32[64,64]{1,0:T(8,128)} %map_ref.3, f32[1280,128]{1,0:T(8,128)} %bitcast.37), custom_call_target="tpu_custom_call" | custom-call | tf_op jit(solution)/shard_map/pivot_cholesky/pallas_call | solution.py:123
  176.5 0.0 collective-permute-done.11
  176.5 2.5 %broadcast_select_fusion.row_ref = f32[512,512]{1,0:T(8,128)} fusion(f32[512,512]{1,0:T(8,128)} %collective-permute-done.11, f32[512,512]{1,0:T(8,128)} %select_select_fusion, pred[]{:T(512)S(6)} %eq.79), kind=kLoop, calls=%fused_computation.3 | loop fusion | flops 262144 | bytes 3145729 | tf_op jit(solution)/shard_map/jit(_where)/select_n | solution.py:267
  178.9 0.0 all-to-all-done.3
  178.9 1.6 copy-done
  180.6 20.3 %schur_update.1 = f32[4,512,512]{2,1,0:T(8,128)} custom-call(s32[2]{0:T(128)} %pad_add_fusion.place_ref, s32[64,64]{1,0:T(8,128)} %map_ref.3, f32[4,512,512]{2,1,0:T(8,128)} %bitcast.34, f32[4,2,4,16,512]{4,3,2,1,0:T(8,128)} %bitcast.36, f32[4,4,2,48,512]{4,3,2,1,0:T(8,128)} %bitcast.35, f32[512,512]{1,0:T(8,128)} %broadcast_select_fusion.row_ref, ...), custom_call_target="tpu_custom_call" | custom-call | tf_op jit(solution)/shard_map/schur_update/pallas_call | solution.py:190
  (14 shorter events, 0.1 us)
Async XLA Ops:
  21.0 6.3 %collective-permute-start.14 = (f32[160,128]{1,0:T(8,128)S(1)}, f32[160,128]{1,0:T(8,128)S(1)}, u32[]{:S(2)}, u32[]{:S(2)}) collective-permute-start(f32[160,128]{1,0:T(8,128)S(1)} %slice_bitcast_fusion.9), channel_id=1, source_target_pairs={{0,8},{1,9},{2,10},{3,11},{4,12},{5,13},{6,14},{7,15}} | collective-permute-start | bytes 245768 | tf_op jit(solution)/shard_map/ppermute | solution.py:233
  22.3 5.7 %collective-permute-start.13 = (f32[160,128]{1,0:T(8,128)S(1)}, f32[160,128]{1,0:T(8,128)S(1)}, u32[]{:S(2)}, u32[]{:S(2)}) collective-permute-start(f32[160,128]{1,0:T(8,128)S(1)} %slice_bitcast_fusion.9), channel_id=1, source_target_pairs={{0,24},{1,25},{2,26},{3,27},{4,28},{5,29},{6,30},{7,31}} | collective-permute-start | bytes 245768 | tf_op jit(solution)/shard_map/ppermute | solution.py:233
  22.9 5.0 %collective-permute-start.12 = (f32[160,128]{1,0:T(8,128)S(1)}, f32[160,128]{1,0:T(8,128)S(1)}, u32[]{:S(2)}, u32[]{:S(2)}) collective-permute-start(f32[160,128]{1,0:T(8,128)S(1)} %slice_bitcast_fusion.9), channel_id=1, source_target_pairs={{0,16},{1,17},{2,18},{3,19},{4,20},{5,21},{6,22},{7,23}} | collective-permute-start | bytes 245768 | tf_op jit(solution)/shard_map/ppermute | solution.py:233
  25.0 12.0 %collective-permute-start.7 = (f32[64,512]{1,0:T(8,128)S(1)}, f32[64,512]{1,0:T(8,128)S(1)}, u32[]{:S(2)}, u32[]{:S(2)}) collective-permute-start(f32[64,512]{1,0:T(8,128)S(1)} %get-tuple-element.9), channel_id=1, source_target_pairs={{0,0},{8,1},{16,2},{24,3},{32,4},{40,5},{48,6},{56,7},{64,64},{72,... | collective-permute-start | bytes 393224 | tf_op jit(solution)/shard_map/ppermute | solution.py:254
  25.7 13.6 %collective-permute-start.6 = (f32[64,512]{1,0:T(8,128)S(1)}, f32[64,512]{1,0:T(8,128)S(1)}, u32[]{:S(2)}, u32[]{:S(2)}) collective-permute-start(f32[64,512]{1,0:T(8,128)S(1)} %get-tuple-element.10), channel_id=1, source_target_pairs={{0,8},{8,9},{16,10},{24,11},{32,12},{40,13},{48,14},{56,15},{64,72... | collective-permute-start | bytes 393224 | tf_op jit(solution)/shard_map/ppermute | solution.py:254
  27.3 12.7 %collective-permute-start.5 = (f32[64,512]{1,0:T(8,128)S(1)}, f32[64,512]{1,0:T(8,128)S(1)}, u32[]{:S(2)}, u32[]{:S(2)}) collective-permute-start(f32[64,512]{1,0:T(8,128)S(1)} %get-tuple-element.11), channel_id=1, source_target_pairs={{0,16},{8,17},{16,18},{24,19},{32,20},{40,21},{48,22},{56,23},{64,... | collective-permute-start | bytes 393224 | tf_op jit(solution)/shard_map/ppermute | solution.py:254
  28.0 12.6 %collective-permute-start.15 = (f32[160,128]{1,0:T(8,128)S(1)}, f32[160,128]{1,0:T(8,128)S(1)}, u32[]{:S(2)}, u32[]{:S(2)}) collective-permute-start(f32[160,128]{1,0:T(8,128)S(1)} %select_select_fusion.3), channel_id=1, source_target_pairs={{0,128},{1,129},{2,130},{3,131},{4,132},{5,133},{6,134},{7,135},{8... | collective-permute-start | bytes 245768 | tf_op jit(solution)/shard_map/ppermute | solution.py:233
  36.2 5.1 %collective-permute-start.4 = (f32[64,512]{1,0:T(8,128)S(1)}, f32[64,512]{1,0:T(8,128)S(1)}, u32[]{:S(2)}, u32[]{:S(2)}) collective-permute-start(f32[64,512]{1,0:T(8,128)S(1)} %get-tuple-element.12), channel_id=1, source_target_pairs={{0,24},{8,25},{16,26},{24,27},{32,28},{40,29},{48,30},{56,31},{64,... | collective-permute-start | bytes 393224 | tf_op jit(solution)/shard_map/ppermute | solution.py:254
  37.0 5.7 %collective-permute-start.3 = (f32[64,512]{1,0:T(8,128)S(1)}, f32[64,512]{1,0:T(8,128)S(1)}, u32[]{:S(2)}, u32[]{:S(2)}) collective-permute-start(f32[64,512]{1,0:T(8,128)S(1)} %get-tuple-element.13), channel_id=1, source_target_pairs={{0,32},{8,33},{16,34},{24,35},{32,36},{40,37},{48,38},{56,39},{64,... | collective-permute-start | bytes 393224 | tf_op jit(solution)/shard_map/ppermute | solution.py:254
  39.3 4.7 %collective-permute-start.2 = (f32[64,512]{1,0:T(8,128)S(1)}, f32[64,512]{1,0:T(8,128)S(1)}, u32[]{:S(2)}, u32[]{:S(2)}) collective-permute-start(f32[64,512]{1,0:T(8,128)S(1)} %get-tuple-element.14), channel_id=1, source_target_pairs={{0,40},{8,41},{16,42},{24,43},{32,44},{40,45},{48,46},{56,47},{64,... | collective-permute-start | bytes 393224 | tf_op jit(solution)/shard_map/ppermute | solution.py:254
  40.0 5.3 %collective-permute-start.1 = (f32[64,512]{1,0:T(8,128)S(1)}, f32[64,512]{1,0:T(8,128)S(1)}, u32[]{:S(2)}, u32[]{:S(2)}) collective-permute-start(f32[64,512]{1,0:T(8,128)S(1)} %get-tuple-element.15), channel_id=1, source_target_pairs={{0,48},{8,49},{16,50},{24,51},{32,52},{40,53},{48,54},{56,55},{64,... | collective-permute-start | bytes 393224 | tf_op jit(solution)/shard_map/ppermute | solution.py:254
  40.7 4.6 %collective-permute-start = (f32[64,512]{1,0:T(8,128)S(1)}, f32[64,512]{1,0:T(8,128)S(1)}, u32[]{:S(2)}, u32[]{:S(2)}) collective-permute-start(f32[64,512]{1,0:T(8,128)S(1)} %get-tuple-element.16), channel_id=1, source_target_pairs={{0,56},{8,57},{16,58},{24,59},{32,60},{40,61},{48,62},{56,63},{64,... | collective-permute-start | bytes 393224 | tf_op jit(solution)/shard_map/ppermute | solution.py:254
  41.4 13.8 %collective-permute-start.18 = (f32[160,128]{1,0:T(8,128)S(1)}, f32[160,128]{1,0:T(8,128)S(1)}, u32[]{:S(2)}, u32[]{:S(2)}) collective-permute-start(f32[160,128]{1,0:T(8,128)S(1)} %broadcast_select_fusion.1), channel_id=1, source_target_pairs={{0,32},{1,33},{2,34},{3,35},{4,36},{5,37},{6,38},{7,39},{8,40},{9,... | collective-permute-start | bytes 245768 | tf_op jit(solution)/shard_map/ppermute | solution.py:233
  42.7 12.4 %collective-permute-start.17 = (f32[160,128]{1,0:T(8,128)S(1)}, f32[160,128]{1,0:T(8,128)S(1)}, u32[]{:S(2)}, u32[]{:S(2)}) collective-permute-start(f32[160,128]{1,0:T(8,128)S(1)} %broadcast_select_fusion.1), channel_id=1, source_target_pairs={{0,224},{1,225},{2,226},{3,227},{4,228},{5,229},{6,230},{7,231},{8... | collective-permute-start | bytes 245768 | tf_op jit(solution)/shard_map/ppermute | solution.py:233
  44.0 11.1 %collective-permute-start.16 = (f32[160,128]{1,0:T(8,128)S(1)}, f32[160,128]{1,0:T(8,128)S(1)}, u32[]{:S(2)}, u32[]{:S(2)}) collective-permute-start(f32[160,128]{1,0:T(8,128)S(1)} %broadcast_select_fusion.1), channel_id=1, source_target_pairs={{0,64},{1,65},{2,66},{3,67},{4,68},{5,69},{6,70},{7,71},{8,72},{9,... | collective-permute-start | bytes 245768 | tf_op jit(solution)/shard_map/ppermute | solution.py:233
  46.1 13.5 %all-to-all-start = ((f32[4,16,512]{2,1,0:T(8,128)}), f32[4,16,512]{2,1,0:T(8,128)S(1)}, u32[]{:S(2)}, u32[]{:S(2)}) async-start(f32[4,16,512]{2,1,0:T(8,128)} %broadcast_in_dim.19), calls=%async_computation | async-start | bytes 262144 | tf_op jit(solution)/shard_map/all_to_all | solution.py:219
  60.5 18.0 %all-to-all-start.5 = ((f32[8,160,128]{2,1,0:T(8,128)}), f32[8,160,128]{2,1,0:T(8,128)S(1)}, u32[]{:S(2)}, u32[]{:S(2)}) async-start(f32[8,160,128]{2,1,0:T(8,128)} %broadcast_in_dim.23), calls=%async_computation.5 | async-start | bytes 1310720 | tf_op jit(solution)/shard_map/all_to_all | solution.py:219
  78.6 27.9 %copy-start.2 = (f32[8,160,128]{2,1,0:T(8,128)}, f32[8,160,128]{2,1,0:T(8,128)S(1)}, u32[]{:S(2)}) copy-start(f32[8,160,128]{2,1,0:T(8,128)S(1)} %all-to-all-done.5) | copy-start | bytes 1966084
  106.4 30.5 %all-to-all-start.1 = ((f32[8,4,16,512]{3,2,1,0:T(8,128)}), f32[8,4,16,512]{3,2,1,0:T(8,128)S(1)}, u32[]{:S(2)}, u32[]{:S(2)}) async-start(f32[8,4,16,512]{3,2,1,0:T(8,128)} %broadcast_in_dim.20), calls=%async_computation.1 | async-start | bytes 2097152 | tf_op jit(solution)/shard_map/all_to_all | solution.py:219
  110.0 34.1 %collective-permute-start.10 = (f32[512,512]{1,0:T(8,128)}, f32[512,512]{1,0:T(8,128)}, u32[]{:S(2)}, u32[]{:S(2)}) collective-permute-start(f32[512,512]{1,0:T(8,128)} %slice_bitcast_fusion), channel_id=1, source_target_pairs={{0,2},{8,10},{16,18},{24,26},{32,34},{40,42},{48,50},{56,58},{64,6... | collective-permute-start | bytes 3145736 | tf_op jit(solution)/shard_map/ppermute | solution.py:263
  111.3 32.8 %collective-permute-start.9 = (f32[512,512]{1,0:T(8,128)}, f32[512,512]{1,0:T(8,128)}, u32[]{:S(2)}, u32[]{:S(2)}) collective-permute-start(f32[512,512]{1,0:T(8,128)} %slice_bitcast_fusion), channel_id=1, source_target_pairs={{0,6},{8,14},{16,22},{24,30},{32,38},{40,46},{48,54},{56,62},{64,7... | collective-permute-start | bytes 3145736 | tf_op jit(solution)/shard_map/ppermute | solution.py:263
  113.0 31.1 %collective-permute-start.8 = (f32[512,512]{1,0:T(8,128)}, f32[512,512]{1,0:T(8,128)}, u32[]{:S(2)}, u32[]{:S(2)}) collective-permute-start(f32[512,512]{1,0:T(8,128)} %slice_bitcast_fusion), channel_id=1, source_target_pairs={{0,4},{8,12},{16,20},{24,28},{32,36},{40,44},{48,52},{56,60},{64,6... | collective-permute-start | bytes 3145736 | tf_op jit(solution)/shard_map/ppermute | solution.py:263
  136.9 2.1 %copy-start.1 = (f32[8,4,16,512]{3,2,1,0:T(8,128)}, f32[8,4,16,512]{3,2,1,0:T(8,128)S(1)}, u32[]{:S(2)}) copy-start(f32[8,4,16,512]{3,2,1,0:T(8,128)S(1)} %all-to-all-done.1) | copy-start | bytes 3145732
  139.0 39.9 %all-to-all-start.3 = ((f32[4,8,48,512]{3,2,1,0:T(8,128)}), f32[4,8,48,512]{3,2,1,0:T(8,128)S(1)}, u32[]{:S(2)}, u32[]{:S(2)}) async-start(f32[4,8,48,512]{3,2,1,0:T(8,128)} %broadcast_in_dim.22), calls=%async_computation.3 | async-start | bytes 6291456 | tf_op jit(solution)/shard_map/all_to_all | solution.py:219
  147.2 29.3 %collective-permute-start.11 = (f32[512,512]{1,0:T(8,128)}, f32[512,512]{1,0:T(8,128)}, u32[]{:S(2)}, u32[]{:S(2)}) collective-permute-start(f32[512,512]{1,0:T(8,128)} %select_select_fusion), channel_id=1, source_target_pairs={{0,1},{2,3},{4,5},{6,7},{8,9},{10,11},{12,13},{14,15},{16,17},{18,... | collective-permute-start | bytes 3145736 | tf_op jit(solution)/shard_map/ppermute | solution.py:266
  178.9 1.6 copy-start

commit v3 on v0

v3 whole, which is shorter than its diff:
```python
import functools

import jax
import jax.numpy as jnp
from jax import lax
from jax.experimental import pallas as pl
from jax.experimental.pallas import tpu as pltpu
from jax.sharding import PartitionSpec as P

BS = 256
N = 512
NB = 128
CHUNK = N // 8
HIGHEST = lax.Precision.HIGHEST
BOTH = ("row", "col")
VMEM = pl.BlockSpec(memory_space=pltpu.VMEM)
SMEM = pl.BlockSpec(memory_space=pltpu.SMEM)


def dot_nn(a, b):
    return lax.dot_general(a, b, (((1,), (0,)), ((), ())), precision=HIGHEST, preferred_element_type=jnp.float32)


def dot_nt(a, b):
    return lax.dot_general(a, b, (((1,), (1,)), ((), ())), precision=HIGHEST, preferred_element_type=jnp.float32)


def spread(row):
    return jnp.broadcast_to(row, (8, NB))


def factor_blocks(d_refs, m_refs):
    sub = lax.broadcasted_iota(jnp.int32, (8, NB), 0)
    lane = lax.broadcasted_iota(jnp.int32, (8, NB), 1)
    for first in range(0, NB, 32):
        tiles_of = [[d_ref[first + 8 * t : first + 8 * t + 8, :] for t in range(4)] for d_ref in d_refs]
        for step in range(4):
            s = first + 8 * step
            here = (lane >= s) & (lane < s + 8)
            state = []
            for tiles in tiles_of:
                cols = [spread(tiles[step][:, s + k : s + k + 1]) for k in range(8)]
                rows = jnp.where(here, jnp.where(lane == sub + s, 1.0, 0.0), tiles[step])
                state.append([cols, rows, jnp.ones_like(rows), rows])
            for j in range(8):
                own = sub == j
                for one in state:
                    cols, rows, diag, kept = one
                    d = cols[j][j : j + 1, :]
                    diag = jnp.where(own, spread(d), diag)
                    factor = jnp.where(own, 0.0, cols[j] * spread(1.0 / d))
                    for k in range(j + 1, 8):
                        cols[k] = cols[k] - factor * spread(cols[k][j : j + 1, :])
                    pivot_row = spread(rows[j : j + 1, :])
                    one[1:] = rows - factor * pivot_row, diag, jnp.where(own, pivot_row, kept)
            for tiles, m_ref, (_, rows, diag, kept) in zip(tiles_of, m_refs, state):
                m_ref[s : s + 8, :] = jnp.where(lane < s + 8, kept * lax.rsqrt(diag), 0.0)
                tiles[step] = rows / diag
                solved = [spread(tiles[step][k : k + 1, :]) for k in range(8)]
                for t in [*range(step + 1, 4), *range(step)]:
                    old = tiles[t]
                    terms = [spread(old[:, s + k : s + k + 1]) * solved[k] for k in range(8)]
                    while len(terms) > 1:
                        terms = [a + b for a, b in zip(terms[::2], terms[1::2])]
                    tiles[t] = jnp.where(here, 0.0, old) - terms[0]
        if first + 32 < NB:
            for tiles, d_ref in zip(tiles_of, d_refs):
                below = d_ref[first + 32 :, :]
                above = [jnp.zeros((first, NB), jnp.float32)] if first else []
                under = [jnp.zeros((NB - first - 32, NB), jnp.float32)]
                column = lax.broadcasted_iota(jnp.int32, below.shape, 1)
                inside = (column >= first) & (column < first + 32)
                product = dot_nn(below, jnp.concatenate(above + tiles + under, axis=0))
                d_ref[first + 32 :, :] = jnp.where(inside, 0.0, below) - product


def panels(groups):
    out, at = [], 0
    for b in range(N // groups // NB):
        for g in range(groups):
            height = N // groups - b * NB
            out.append((g, b, at, height))
            at += height
    return out


def packed_rows(groups):
    return sum(height for _, _, _, height in panels(groups))


def pivot_kernel(groups, place_ref, *refs):
    share_refs, (l_ref, inv_ref, w_ref, x_ref, d_ref, m_ref) = refs[:4], refs[4:]
    n = N // groups
    share = packed_rows(groups) // 4
    x = place_ref[1] // 2
    for step, ref in zip((0, 1, 3, 2), share_refs):
        w_ref[pl.ds(pl.multiple_of(lax.rem(x + step, 4) * share, 8), share), :] = ref[...]
    starts = {(g, b): (at, height) for g, b, at, height in panels(groups)}
    row_ids = lax.broadcasted_iota(jnp.int32, (n, n), 0)
    col_ids = lax.broadcasted_iota(jnp.int32, (n, n), 1)
    for g in range(groups):
        x_ref[g] = jnp.where(row_ids == col_ids, 1.0, 0.0).astype(jnp.float32)
    for b in range(n // NB):
        o, e = b * NB, (b + 1) * NB
        for g in range(groups):
            d_ref[g] = w_ref[pl.ds(starts[g, b][0], NB), :]
        factor_blocks([d_ref.at[g] for g in range(groups)], [m_ref.at[g] for g in range(groups)])
        for g in range(groups):
            at, height = starts[g, b]
            m = m_ref[g]
            low = dot_nt(w_ref[at : at + height, :], m)
            if e < n:
                for k in range(b + 1, n // NB):
                    rest = low[(k - b) * NB :]
                    to, rows = starts[g, k]
                    w_ref[to : to + rows, :] -= dot_nt(rest, rest[:NB])
            tri = lax.broadcasted_iota(jnp.int32, low.shape, 0) >= lax.broadcasted_iota(jnp.int32, low.shape, 1)
            l_ref[g, o:, o:e] = jnp.where(tri, low, 0.0)
            inv = dot_nn(m, x_ref[g, o:e, :e])
            inv_ref[g, o:e, :e] = inv
            if b:
                l_ref[g, :o, o:e] = jnp.zeros((o, NB), jnp.float32)
            if e < n:
                inv_ref[g, o:e, e:] = jnp.zeros((NB, n - e), jnp.float32)
                x_ref[g, e:, :e] -= dot_nn(low[NB:], inv)


def pivot(groups, place, shares):
    n = N // groups
    return pl.pallas_call(
        functools.partial(pivot_kernel, groups),
        out_shape=(jax.ShapeDtypeStruct((groups, n, n), jnp.float32),) * 2,
        in_specs=[SMEM] + [VMEM] * 4,
        out_specs=(VMEM, VMEM),
        scratch_shapes=[
            pltpu.VMEM((packed_rows(groups), NB), jnp.float32),
            pltpu.VMEM((groups, n, n), jnp.float32),
            pltpu.VMEM((groups, NB, NB), jnp.float32),
            pltpu.VMEM((groups, NB, NB), jnp.float32),
        ],
        name="pivot_cholesky",
    )(place, *shares)


def prepare_kernel(groups, place_ref, map_ref, head_ref, *out_refs):
    share_refs, chunk_refs, panel_ref = out_refs[:4], out_refs[4:12], out_refs[12]
    p = place_ref[0]
    n = N // groups
    for a in range(2):
        rows = slice(a * BS, (a + 1) * BS)
        panel = head_ref[0, rows, :n] * map_ref[2 * p + a, 0].astype(jnp.float32)
        if groups == 2:
            panel = panel + head_ref[0, rows, n:] * map_ref[2 * p + a, 1].astype(jnp.float32)
        panel_ref[rows, :] = panel
        for t in range(4):
            chunk_refs[4 * a + t][...] = panel[t * CHUNK : (t + 1) * CHUNK]
    lower = []
    for g, b, _, height in panels(groups):
        first = g * n + b * NB
        lower.append(head_ref[0, first : first + height, first : first + NB])
    lower = jnp.concatenate(lower, axis=0)
    share = packed_rows(groups) // 4
    for x in range(4):
        share_refs[x][...] = lower[x * share : (x + 1) * share]


def prepare(groups, place, block_map, front):
    n = N // groups
    shapes = [(packed_rows(groups) // 4, NB)] * 4 + [(CHUNK, n)] * 8 + [(N, n)]
    return pl.pallas_call(
        functools.partial(prepare_kernel, groups),
        grid=(1,),
        out_shape=tuple(jax.ShapeDtypeStruct(s, jnp.float32) for s in shapes),
        in_specs=[SMEM, SMEM, pl.BlockSpec((1, N, N), lambda i: (0, 0, 0))],
        out_specs=tuple(pl.BlockSpec(s, lambda i: (0, 0)) for s in shapes),
        name="prepare",
    )(place, block_map, front)


def update_kernel(groups, place_ref, map_ref, front_ref, col_ref, row_ref, l_ref, inv_ref, out_ref, row_factor_ref):
    c = pl.program_id(0)
    p, q = place_ref[0], place_ref[1]
    j = c * 8 + q
    n = N // groups

    def marked(r, s):
        return map_ref[r, s] != 0

    def in_panel(r):
        return marked(r, 0) | marked(r, 1)

    def inverse(r):
        return inv_ref[map_ref[r, 1]] if groups == 2 else inv_ref[0]

    @pl.when(c == 0)
    def _():
        for a in range(2):
            rows = slice(a * BS, (a + 1) * BS)
            row_factor_ref[rows, :] = dot_nt(row_ref[rows, :], inverse(2 * p + a))

    @pl.when((p > 0) & (j > 0))
    def _():
        for b in range(2):
            s = 2 * j + b
            cols = slice(b * BS, (b + 1) * BS)
            touched = [marked(2 * p + a, s) & in_panel(s) for a in range(2)]

            @pl.when(touched[0] | touched[1])
            def _():
                block = jnp.concatenate([col_ref[t, 0, b] for t in range(4)], axis=0)
                factor = dot_nt(block, inverse(s))
                for a in range(2):

                    @pl.when(touched[a])
                    def _():
                        rows = slice(a * BS, (a + 1) * BS)
                        out_ref[0, rows, cols] = front_ref[0, rows, cols] - dot_nt(row_factor_ref[rows, :], factor)

            for a in range(2):

                @pl.when(jnp.logical_not(touched[a]))
                def _():
                    rows = slice(a * BS, (a + 1) * BS)
                    weight = map_ref[2 * p + a, s].astype(jnp.float32)
                    out_ref[0, rows, cols] = front_ref[0, rows, cols] * weight

    @pl.when((p > 0) & (j == 0))
    def _():
        for a in range(2):
            rows = slice(a * BS, (a + 1) * BS)
            if groups == 1:
                out_ref[0, rows, :] = row_factor_ref[rows, :]
            else:
                for b in range(2):
                    weight = map_ref[2 * p + a, b].astype(jnp.float32)
                    out_ref[0, rows, b * BS : (b + 1) * BS] = row_factor_ref[rows, :] * weight

    @pl.when((p == 0) & (j > 0))
    def _():
        out_ref[0] = jnp.zeros((N, N), jnp.float32)

    @pl.when((p == 0) & (j == 0))
    def _():
        out_ref[0] = jnp.zeros((N, N), jnp.float32)
        for g in range(groups):
            out_ref[0, g * n : (g + 1) * n, g * n : (g + 1) * n] = l_ref[g]


def update(groups, place, block_map, front, cols, rows, low, inv):
    n = N // groups
    tile = pl.BlockSpec((1, N, N), lambda c: (c, 0, 0))
    square = pl.BlockSpec((groups, n, n), lambda c: (0, 0, 0))
    return pl.pallas_call(
        functools.partial(update_kernel, groups),
        grid=(front.shape[0],),
        out_shape=jax.ShapeDtypeStruct(front.shape, jnp.float32),
        in_specs=[
            SMEM,
            SMEM,
            tile,
            pl.BlockSpec((4, 1, 2, CHUNK, n), lambda c: (0, c, 0, 0, 0)),
            pl.BlockSpec((N, n), lambda c: (0, 0)),
            square,
            square,
        ],
        out_specs=tile,
        scratch_shapes=[pltpu.VMEM((N, n), jnp.float32)],
        name="schur_update",
    )(place, block_map, front, cols, rows, low, inv)


def device(z, y, x, core):
    return ((z % 8 * 4 + y % 4) * 4 + x % 4) * 2 + core


Y_GROUPS = [[z * 4 + y for y in range(4)] for z in range(8)]
Z_GROUPS = [[z * 4 + y for z in range(8)] for y in range(4)]
XS, YS, ZS = range(4), range(4), range(8)


def gather(value, axis, size, groups=None):
    return lax.all_to_all(jnp.broadcast_to(value, (size, *value.shape)), axis, 0, 0, axis_index_groups=groups)


def send(value, pairs):
    return lax.ppermute(value, BOTH, pairs)


def receive(value, arrived):
    for hit, got in arrived:
        value = jnp.where(hit, got, value)
    return value


def run(groups, front, block_map):
    p = lax.axis_index("row")
    q = lax.axis_index("col")
    z, y, x, core = p // 4, p % 4, q // 2, q % 2
    place = jnp.stack([p, q]).astype(jnp.int32)
    *sent, panel = prepare(groups, place, block_map, front)
    shares, chunks = sent[:4], sent[4:]

    arrived = [(x == d, send(shares[d], [(device(0, 0, 0, 0), device(0, 0, d, 0))])) for d in (1, 3, 2)]
    share = receive(shares[0], arrived)
    pieces = [send(chunks[t], [(s * 8, (s // 8 * 8 + t) * 8 + s % 8) for s in range(32)]) for t in range(8)]
    arrived = [
        (y == d, send(share, [(device(0, 0, i, 0), device(0, d, i, 0)) for i in XS])) for d in (1, 3, 2)
    ]
    share = receive(share, arrived)
    arrived = [(z == 4, send(share, [(device(0, j, i, 0), device(4, j, i, 0)) for j in YS for i in XS]))]
    share = receive(share, arrived)
    arrived = [
        (z % 4 == d % 4, send(share, [(device(k, j, i, 0), device(k + d, j, i, 0)) for k in (0, 4) for j in YS for i in XS]))
        for d in (1, 7, 2)
    ]
    share = receive(share, arrived)
    piece = receive(pieces[0], [(p % 8 == t, pieces[t]) for t in range(1, 8)])
    cols = gather(gather(piece, "row", 8, Z_GROUPS), "row", 4, Y_GROUPS).reshape(4, 4, 2, CHUNK, N // groups)
    quarters = [share] + [
        send(share, [(device(k, j, i + d, 0), device(k, j, i, 0)) for k in ZS for j in YS for i in XS]) for d in (1, 3, 2)
    ]
    swap = [(device(k, j, i, 0), device(k, j, i, 1)) for k in ZS for j in YS for i in XS]
    quarters = [jnp.where(core == 1, send(one, swap), one) for one in quarters]
    arrived = [
        (x == d, send(panel, [(device(k, j, 0, 0), device(k, j, d, 0)) for k in ZS for j in YS])) for d in (1, 3, 2)
    ]
    row = receive(panel, arrived)
    row = jnp.where(core == 1, send(row, swap), row)

    low, inv = pivot(groups, place, quarters)
    return update(groups, place, block_map, front, cols, row, low, inv)


def body(front_matrix, block_map):
    front = front_matrix[0, 0, :, 0]
    out = lax.cond(
        block_map[0, 1] != 0,
        functools.partial(run, 1),
        functools.partial(run, 2),
        front,
        block_map,
    )
    return out.reshape(front_matrix.shape)


def solution(mesh):
    return jax.shard_map(
        body,
        mesh=mesh,
        in_specs=(P(None, "row", None, "col", None, None), P()),
        out_specs=P(None, "row", None, "col", None, None),
        check_vma=False,
    )
```

time: 592 us -> 120 us (0.20)
  waiting for transfers between devices: 386 us -> 15 us
  other arithmetic: 139 us -> 5.38 us
  starting transfers between devices: 0.09 us -> 68.1 us
  local copies, waits for them, and re-layouts: 31 us -> 4.99 us
  Pallas kernels: 0 us -> 24.6 us
  between operations: 16.2 us -> 0.66 us
  matrix products: 14.4 us -> 0 us
    psum x3 -> x0, waiting for transfers between devices: 386 us -> none  [spread(): return lax.psum(kept, axis)]
    another operation x17 -> x1, other arithmetic: 119 us -> 0.56 us  [run(): place = jnp.stack([p, q]).astype(jnp.int32)]
    ppermute x0 -> x29, starting transfers between devices: none -> 52 us  [send(): return lax.ppermute(value, BOTH, pairs)]
    pallas_call x0 -> x3, Pallas kernels: none -> 24.6 us  [the longest x1 13.3 us: pivot(): pl.pallas_call(functools.partial(pivot_kernel, groups), out_shape=(jax.Sh...]
    all_to_all x0 -> x2, starting transfers between devices: none -> 16.1 us  [gather(): lax.all_to_all(jnp.broadcast_to(value, (size, *value.shape)), axis, 0, 0,...]
    ppermute x0 -> x29, waiting for transfers between devices: none -> 15 us  [send(): return lax.ppermute(value, BOTH, pairs)]
    mul x3 -> x0, local copies, waits for them, and re-layouts: 9.69 us -> none  [body(): front_matrix.reshape(row_blocks, col_blocks, halves, BS, halves, BS)]
    dot_general x1 -> x0, matrix products: 9.43 us -> none  [body(): jnp.einsum('axk,cyk->acxy', row_update, col_update, precision=HIGHEST_PRE...]
  transfers between devices with their start and end apart: 3 -> 31, of which waited for: 3 -> 3; matrix products, arithmetic and copies ran while one was open for 0% -> 6% of each run, Pallas kernels for 0% -> 11%
where the time goes in v3:
time: 120 us; the launch traced here: 119 us
  starting transfers between devices  68.1 us (57%)
  Pallas kernels  24.6 us (20%)
  waiting for transfers between devices  15 us (12%)
  other arithmetic  5.38 us (4%)
  local copies, waits for them, and re-layouts  4.99 us (4%)
    ppermute x29, starting transfers between devices, send(): return lax.ppermute(value, BOTH, pairs)  52 us
    all_to_all x2, starting transfers between devices, gather(): lax.all_to_all(jnp.broadcast_to(value, (size, *value.shape)), axis, 0, 0,...  16.1 us
    ppermute x29, waiting for transfers between devices, send(): return lax.ppermute(value, BOTH, pairs)  15 us
    pallas_call x1, Pallas kernels, pivot(): pl.pallas_call(functools.partial(pivot_kernel, groups), out_shape=(jax.Sh...  13.3 us
    pallas_call x1, Pallas kernels, update(): pl.pallas_call(functools.partial(update_kernel, groups), grid=(front.shap...  8.87 us
    select_n x4, other arithmetic, run(): quarters = [jnp.where(core == 1, send(one, swap), one) for one in quarters]  2.64 us
    broadcast_in_dim x2, local copies, waits for them, and re-layouts, gather(): jnp.broadcast_to(value, (size, *value.shape))  2.4 us
  transfers between devices with their start and end apart: 31, of which 3 were waited for; matrix products, arithmetic and copies ran while one was open for 6% of the time, Pallas kernels for 11%

profile of v3, /device:TPU:10, one launch (start us, length us, event | category | flops | bytes accessed | tf_op | source)
XLA Modules:
  0.0 119.3 jit_solution(3925008795522113148)
XLA Ops:
  0.0 1.3 %slice.3 = s32[1,1]{1,0:T(1,128)} slice(s32[64,64]{1,0:T(8,128)} %param.5), slice={[0:1], [1:2]} | slice | bytes 8 | tf_op jit(solution)/shard_map/slice | solution.py:337
  1.9 117.3 %conditional.1 = (f32[1,1,4,1,512,512]{5,4,3,2,1,0:T(8,128)}) conditional(s32[]{:T(128)} %bitcast.18, (s32[64,64]{1,0:T(8,128)}, f32[1,1,4,1,512,512]{5,4,3,2,1,0:T(8,128)}) %tuple.13, (s32[64,64]{1,0:T(8,128)}, f32[1,1,4,1,512,512]{5,4,3,2,1,0:T(8,128)}) %tuple.13), branch_computations={%region_0.1_spmd, %region_1.2_spmd} | conditional | flops 1851474 | bytes 81135832 | solution.py:336
  1.9 0.6 pad_add_fusion.place_ref
  2.5 2.4 %prepare.2 = (f32[192,128]{1,0:T(8,128)}, f32[192,128]{1,0:T(8,128)}, f32[192,128]{1,0:T(8,128)}, f32[192,128]{1,0:T(8,128)}, f32[64,256]{1,0:T(8,128)}, /*index...) custom-call(s32[2]{0:T(128)} %pad_add_fusion.place_ref, ...), custom_call_target="tpu_custom_call" | custom-call | tf_op jit(solution)/shard_map/cond/branch_0_fun/prepare/pallas_call | solution.py:170
  4.9 0.7 collective-permute-start
  5.5 0.7 collective-permute-start.12
  6.2 0.7 collective-permute-start.13
  6.9 0.7 collective-permute-start.14
  7.6 0.7 collective-permute-start.1
  8.2 0.7 collective-permute-start.2
  9.0 0.7 collective-permute-start.3
  9.6 0.0 collective-permute-done.2
  9.6 0.7 collective-permute-start.4
  10.3 0.0 collective-permute-done.12
  10.3 0.7 collective-permute-start.5
  11.0 0.0 collective-permute-done.13
  11.0 1.3 %collective-permute-start.6 = (f32[64,256]{1,0:T(8,128)}, f32[64,256]{1,0:T(8,128)S(1)}, u32[]{:S(2)}, u32[]{:S(2)}) collective-permute-start(f32[64,256]{1,0:T(8,128)} %get-tuple-element.25), channel_id=1, source_target_pairs={{0,8},{8,9},{16,10},{24,11},{32,12},{40,13},{48,14},{56,15},{64,72... | collective-permute-start | bytes 196616 | tf_op jit(solution)/shard_map/cond/branch_0_fun/ppermute | solution.py:286
  12.3 0.7 collective-permute-start.7
  13.0 0.7 collective-permute-start.15
  13.7 0.0 collective-permute-done.4
  13.7 0.7 collective-permute-start.16
  14.4 0.0 collective-permute-done.5
  14.4 1.3 %collective-permute-start.17 = (f32[192,128]{1,0:T(8,128)S(1)}, f32[192,128]{1,0:T(8,128)S(1)}, u32[]{:S(2)}, u32[]{:S(2)}) collective-permute-start(f32[192,128]{1,0:T(8,128)S(1)} %select_select_fusion.3), channel_id=1, source_target_pairs={{0,8},{2,10},{4,12},{6,14}} | collective-permute-start | bytes 294920 | tf_op jit(solution)/shard_map/cond/branch_0_fun/ppermute | solution.py:286
  15.7 10.1 %collective-permute-done.6 = f32[64,256]{1,0:T(8,128)S(1)} collective-permute-done((f32[64,256]{1,0:T(8,128)}, f32[64,256]{1,0:T(8,128)S(1)}, u32[]{:S(2)}, u32[]{:S(2)}) %collective-permute-start.6) | collective-permute-done | bytes 65568 | tf_op jit(solution)/shard_map/cond/branch_0_fun/ppermute | solution.py:286
  25.8 0.0 collective-permute-done.7
  25.9 0.8 broadcast_in_dim.8
  26.7 7.6 %all-to-all-start = ((f32[8,64,256]{2,1,0:T(8,128)}), f32[8,64,256]{2,1,0:T(8,128)S(1)}, u32[]{:S(2)}, u32[]{:S(2)}) async-start(f32[8,64,256]{2,1,0:T(8,128)} %broadcast_in_dim.8), calls=%async_computation | async-start | bytes 1048576 | tf_op jit(solution)/shard_map/cond/branch_0_fun/all_to_all | solution.py:282
  34.3 0.0 collective-permute-done.15
  34.3 0.0 collective-permute-done.16
  34.3 8.0 %collective-permute-start.18 = (f32[192,128]{1,0:T(8,128)S(1)}, f32[192,128]{1,0:T(8,128)S(1)}, u32[]{:S(2)}, u32[]{:S(2)}) collective-permute-start(f32[192,128]{1,0:T(8,128)S(1)} %select_select_fusion.2), channel_id=1, source_target_pairs={{0,128},{2,130},{4,132},{6,134},{8,136},{10,138},{12,140},{14,142}... | collective-permute-start | bytes 294920 | tf_op jit(solution)/shard_map/cond/branch_0_fun/ppermute | solution.py:286
  42.3 2.8 %collective-permute-done.18 = f32[192,128]{1,0:T(8,128)S(1)} collective-permute-done((f32[192,128]{1,0:T(8,128)S(1)}, f32[192,128]{1,0:T(8,128)S(1)}, u32[]{:S(2)}, u32[]{:S(2)}) %collective-permute-start.18) | collective-permute-done | bytes 98336 | tf_op jit(solution)/shard_map/cond/branch_0_fun/ppermute | solution.py:286
  45.1 1.3 %collective-permute-start.19 = (f32[192,128]{1,0:T(8,128)S(1)}, f32[192,128]{1,0:T(8,128)S(1)}, u32[]{:S(2)}, u32[]{:S(2)}) collective-permute-start(f32[192,128]{1,0:T(8,128)S(1)} %broadcast_select_fusion.1), channel_id=1, source_target_pairs={{0,64},{2,66},{4,68},{6,70},{8,72},{10,74},{12,76},{14,78},{16,80}... | collective-permute-start | bytes 294920 | tf_op jit(solution)/shard_map/cond/branch_0_fun/ppermute | solution.py:286
  46.4 1.3 %collective-permute-start.20 = (f32[192,128]{1,0:T(8,128)S(1)}, f32[192,128]{1,0:T(8,128)S(1)}, u32[]{:S(2)}, u32[]{:S(2)}) collective-permute-start(f32[192,128]{1,0:T(8,128)S(1)} %broadcast_select_fusion.1), channel_id=1, source_target_pairs={{0,224},{2,226},{4,228},{6,230},{8,232},{10,234},{12,236},{14,238}... | collective-permute-start | bytes 294920 | tf_op jit(solution)/shard_map/cond/branch_0_fun/ppermute | solution.py:286
  47.7 1.3 %collective-permute-start.21 = (f32[192,128]{1,0:T(8,128)S(1)}, f32[192,128]{1,0:T(8,128)S(1)}, u32[]{:S(2)}, u32[]{:S(2)}) collective-permute-start(f32[192,128]{1,0:T(8,128)S(1)} %broadcast_select_fusion.1), channel_id=1, source_target_pairs={{0,32},{2,34},{4,36},{6,38},{8,40},{10,42},{12,44},{14,46},{16,48}... | collective-permute-start | bytes 294920 | tf_op jit(solution)/shard_map/cond/branch_0_fun/ppermute | solution.py:286
  49.0 0.7 collective-permute-start.8
  49.7 1.5 %collective-permute-start.9 = (f32[512,256]{1,0:T(8,128)}, f32[512,256]{1,0:T(8,128)}, u32[]{:S(2)}, u32[]{:S(2)}) collective-permute-start(f32[512,256]{1,0:T(8,128)} %get-tuple-element.27), channel_id=1, source_target_pairs={{0,6},{8,14},{16,22},{24,30},{32,38},{40,46},{48,54},{56,62},{64,7... | collective-permute-start | bytes 1572872 | tf_op jit(solution)/shard_map/cond/branch_0_fun/ppermute | solution.py:286
  51.2 1.3 %collective-permute-start.10 = (f32[512,256]{1,0:T(8,128)}, f32[512,256]{1,0:T(8,128)}, u32[]{:S(2)}, u32[]{:S(2)}) collective-permute-start(f32[512,256]{1,0:T(8,128)} %get-tuple-element.27), channel_id=1, source_target_pairs={{0,2},{8,10},{16,18},{24,26},{32,34},{40,42},{48,50},{56,58},{64,6... | collective-permute-start | bytes 1572872 | tf_op jit(solution)/shard_map/cond/branch_0_fun/ppermute | solution.py:286
  52.5 0.0 collective-permute-done.20
  52.5 0.0 collective-permute-done.21
  52.6 1.9 %collective-permute-start.22 = (f32[192,128]{1,0:T(8,128)S(1)}, f32[192,128]{1,0:T(8,128)}, u32[]{:S(2)}, u32[]{:S(2)}) collective-permute-start(f32[192,128]{1,0:T(8,128)S(1)} %select_select_fusion.1), channel_id=1, source_target_pairs={{0,1},{2,3},{4,5},{6,7},{8,9},{10,11},{12,13},{14,15},{16,17},{18,... | collective-permute-start | bytes 294920 | tf_op jit(solution)/shard_map/cond/branch_0_fun/ppermute | solution.py:286
  54.5 13.0 %collective-permute-start.23 = (f32[192,128]{1,0:T(8,128)S(1)}, f32[192,128]{1,0:T(8,128)S(1)}, u32[]{:S(2)}, u32[]{:S(2)}) collective-permute-start(f32[192,128]{1,0:T(8,128)S(1)} %select_select_fusion.1), channel_id=1, source_target_pairs={{2,0},{4,2},{6,4},{0,6},{10,8},{12,10},{14,12},{8,14},{18,16},{20,... | collective-permute-start | bytes 294920 | tf_op jit(solution)/shard_map/cond/branch_0_fun/ppermute | solution.py:286
  67.5 0.0 all-to-all-done
  67.5 1.6 %broadcast_in_dim.9 = f32[4,8,64,256]{3,2,1,0:T(8,128)} broadcast(f32[8,64,256]{2,1,0:T(8,128)S(1)} %all-to-all-done), dimensions={1,2,3} | broadcast | bytes 2621440 | tf_op jit(solution)/shard_map/cond/branch_0_fun/broadcast_in_dim | solution.py:282
  69.1 8.5 %all-to-all-start.1 = ((f32[4,8,64,256]{3,2,1,0:T(8,128)}), f32[4,8,64,256]{3,2,1,0:T(8,128)S(1)}, u32[]{:S(2)}, u32[]{:S(2)}) async-start(f32[4,8,64,256]{3,2,1,0:T(8,128)} %broadcast_in_dim.9), calls=%async_computation.1 | async-start | bytes 4194304 | tf_op jit(solution)/shard_map/cond/branch_0_fun/all_to_all | solution.py:282
  77.6 1.9 %collective-permute-start.25 = (f32[192,128]{1,0:T(8,128)S(1)}, f32[192,128]{1,0:T(8,128)S(1)}, u32[]{:S(2)}, u32[]{:S(2)}) collective-permute-start(f32[192,128]{1,0:T(8,128)S(1)} %select_select_fusion.1), channel_id=1, source_target_pairs={{6,0},{0,2},{2,4},{4,6},{14,8},{8,10},{10,12},{12,14},{22,16},{16,... | collective-permute-start | bytes 294920 | tf_op jit(solution)/shard_map/cond/branch_0_fun/ppermute | solution.py:286
  79.5 0.0 collective-permute-done.23
  79.5 4.0 %collective-permute-start.27 = (f32[192,128]{1,0:T(8,128)S(1)}, f32[192,128]{1,0:T(8,128)S(1)}, u32[]{:S(2)}, u32[]{:S(2)}) collective-permute-start(f32[192,128]{1,0:T(8,128)S(1)} %select_select_fusion.1), channel_id=1, source_target_pairs={{4,0},{6,2},{0,4},{2,6},{12,8},{14,10},{8,12},{10,14},{20,16},{22,... | collective-permute-start | bytes 294920 | tf_op jit(solution)/shard_map/cond/branch_0_fun/ppermute | solution.py:286
  83.5 0.7 broadcast_select_fusion.5.refs_0_
  84.2 0.0 collective-permute-done.25
  84.2 1.3 %collective-permute-start.24 = (f32[192,128]{1,0:T(8,128)S(1)}, f32[192,128]{1,0:T(8,128)S(1)}, u32[]{:S(2)}, u32[]{:S(2)}) collective-permute-start(f32[192,128]{1,0:T(8,128)S(1)} %collective-permute-done.23), channel_id=1, source_target_pairs={{0,1},{2,3},{4,5},{6,7},{8,9},{10,11},{12,13},{14,15},{16,17},{18,... | collective-permute-start | bytes 294920 | tf_op jit(solution)/shard_map/cond/branch_0_fun/ppermute | solution.py:286
  85.5 2.1 %collective-permute-done.27 = f32[192,128]{1,0:T(8,128)S(1)} collective-permute-done((f32[192,128]{1,0:T(8,128)S(1)}, f32[192,128]{1,0:T(8,128)S(1)}, u32[]{:S(2)}, u32[]{:S(2)}) %collective-permute-start.27) | collective-permute-done | bytes 98336 | tf_op jit(solution)/shard_map/cond/branch_0_fun/ppermute | solution.py:286
  87.5 1.3 %collective-permute-start.26 = (f32[192,128]{1,0:T(8,128)S(1)}, f32[192,128]{1,0:T(8,128)S(1)}, u32[]{:S(2)}, u32[]{:S(2)}) collective-permute-start(f32[192,128]{1,0:T(8,128)S(1)} %collective-permute-done.25), channel_id=1, source_target_pairs={{0,1},{2,3},{4,5},{6,7},{8,9},{10,11},{12,13},{14,15},{16,17},{18,... | collective-permute-start | bytes 294920 | tf_op jit(solution)/shard_map/cond/branch_0_fun/ppermute | solution.py:286
  88.9 1.3 %collective-permute-start.28 = (f32[192,128]{1,0:T(8,128)S(1)}, f32[192,128]{1,0:T(8,128)S(1)}, u32[]{:S(2)}, u32[]{:S(2)}) collective-permute-start(f32[192,128]{1,0:T(8,128)S(1)} %collective-permute-done.27), channel_id=1, source_target_pairs={{0,1},{2,3},{4,5},{6,7},{8,9},{10,11},{12,13},{14,15},{16,17},{18,... | collective-permute-start | bytes 294920 | tf_op jit(solution)/shard_map/cond/branch_0_fun/ppermute | solution.py:286
  90.2 0.0 collective-permute-done.10
  90.2 1.2 %select_select_fusion = f32[512,256]{1,0:T(8,128)S(1)} fusion(f32[512,256]{1,0:T(8,128)} %copy-done.6, f32[512,256]{1,0:T(8,128)} %collective-permute-done.9, f32[512,256]{1,0:T(8,128)} %collective-permute-done.10, f32[512,256]{1,0:T(8,128)S(1)} %copy-done.5, pred[]{:T(512)S(6)} %eq.121, pred[]{:T(512)S(6)} %eq.120, pred[]{:T(512)S(6)} %eq.119), kind=kLoop, calls=%fused_computation | loop fusion | flops 393216 | bytes 2621443 | tf_op jit(solution)/shard_map/cond/branch_0_fun/jit(_where)/select_n | solution.py:291
  91.4 1.5 %collective-permute-start.11 = (f32[512,256]{1,0:T(8,128)S(1)}, f32[512,256]{1,0:T(8,128)S(1)}, u32[]{:S(2)}, u32[]{:S(2)}) collective-permute-start(f32[512,256]{1,0:T(8,128)S(1)} %select_select_fusion), channel_id=1, source_target_pairs={{0,1},{2,3},{4,5},{6,7},{8,9},{10,11},{12,13},{14,15},{16,17},{18,... | collective-permute-start | bytes 1572872 | tf_op jit(solution)/shard_map/cond/branch_0_fun/ppermute | solution.py:286
  92.9 0.7 broadcast_select_fusion.4.refs_1_
  93.6 0.6 broadcast_select_fusion.3.refs_2_
  94.2 0.0 collective-permute-done.28
  94.2 0.7 broadcast_select_fusion.2.refs_3_
  94.9 13.3 %pivot_cholesky.2 = (f32[2,256,256]{2,1,0:T(8,128)}, f32[2,256,256]{2,1,0:T(8,128)}) custom-call(s32[2]{0:T(128)} %pad_add_fusion.place_ref, f32[192,128]{1,0:T(8,128)} %broadcast_select_fusion.5.refs_0_, f32[192,128]{1,0:T(8,128)} %broadcast_select_fusion.4.refs_1_, f32[192,128]{1,0:T(8,128)} %broadcast_select_fusion.3.refs_2_, ...), custom_call_target="tpu_custom_call" | custom-call | tf_op jit(solution)/shard_map/cond/branch_0_fun/pivot_cholesky/pallas_call | solution.py:130
  108.2 0.9 broadcast_select_fusion.row_ref
  109.1 1.3 %copy-done = f32[4,8,64,256]{3,2,1,0:T(8,128)} copy-done((f32[4,8,64,256]{3,2,1,0:T(8,128)}, f32[4,8,64,256]{3,2,1,0:T(8,128)S(1)}, u32[]{:S(2)}) %copy-start) | copy-done | bytes 2097176 | tf_op jit(solution)/shard_map/cond
  110.4 8.9 %schur_update.2 = f32[4,512,512]{2,1,0:T(8,128)} custom-call(s32[2]{0:T(128)} %pad_add_fusion.place_ref, s32[64,64]{1,0:T(8,128)S(1)} %copy-done.3, f32[4,512,512]{2,1,0:T(8,128)} %bitcast.20, f32[4,4,2,64,256]{4,3,2,1,0:T(8,128)} %bitcast.23, f32[512,256]{1,0:T(8,128)} %broadcast_select_fusion.row_ref, f32[2,256,256]{2,1,0:T(8,128)} %get-tuple-element.32.l_ref, ...), custom_call_target="tpu_custom_call" | custom-call | tf_op jit(solution)/shard_map/cond/branch_0_fun/schur_update/pallas_call | solution.py:253
  (25 shorter events, 0.2 us)
Async XLA Ops:
  4.9 3.4 %collective-permute-start = (f32[64,256]{1,0:T(8,128)}, f32[64,256]{1,0:T(8,128)S(1)}, u32[]{:S(2)}, u32[]{:S(2)}) collective-permute-start(f32[64,256]{1,0:T(8,128)} %get-tuple-element.19), channel_id=1, source_target_pairs={{0,56},{8,57},{16,58},{24,59},{32,60},{40,61},{48,62},{56,63},{64,... | collective-permute-start | bytes 196616 | tf_op jit(solution)/shard_map/cond/branch_0_fun/ppermute | solution.py:286
  5.5 4.8 %collective-permute-start.12 = (f32[192,128]{1,0:T(8,128)}, f32[192,128]{1,0:T(8,128)S(1)}, u32[]{:S(2)}, u32[]{:S(2)}) collective-permute-start(f32[192,128]{1,0:T(8,128)} %get-tuple-element.28), channel_id=1, source_target_pairs={{0,4}} | collective-permute-start | bytes 294920 | tf_op jit(solution)/shard_map/cond/branch_0_fun/ppermute | solution.py:286
  6.2 4.8 %collective-permute-start.13 = (f32[192,128]{1,0:T(8,128)}, f32[192,128]{1,0:T(8,128)S(1)}, u32[]{:S(2)}, u32[]{:S(2)}) collective-permute-start(f32[192,128]{1,0:T(8,128)} %get-tuple-element.29), channel_id=1, source_target_pairs={{0,6}} | collective-permute-start | bytes 294920 | tf_op jit(solution)/shard_map/cond/branch_0_fun/ppermute | solution.py:286
  6.9 5.4 %collective-permute-start.14 = (f32[192,128]{1,0:T(8,128)}, f32[192,128]{1,0:T(8,128)S(1)}, u32[]{:S(2)}, u32[]{:S(2)}) collective-permute-start(f32[192,128]{1,0:T(8,128)} %get-tuple-element.30), channel_id=1, source_target_pairs={{0,2}} | collective-permute-start | bytes 294920 | tf_op jit(solution)/shard_map/cond/branch_0_fun/ppermute | solution.py:286
  7.6 1.4 %collective-permute-start.1 = (f32[64,256]{1,0:T(8,128)}, f32[64,256]{1,0:T(8,128)S(1)}, u32[]{:S(2)}, u32[]{:S(2)}) collective-permute-start(f32[64,256]{1,0:T(8,128)} %get-tuple-element.20), channel_id=1, source_target_pairs={{0,48},{8,49},{16,50},{24,51},{32,52},{40,53},{48,54},{56,55},{64,... | collective-permute-start | bytes 196616 | tf_op jit(solution)/shard_map/cond/branch_0_fun/ppermute | solution.py:286
  8.2 1.4 %collective-permute-start.2 = (f32[64,256]{1,0:T(8,128)}, f32[64,256]{1,0:T(8,128)S(1)}, u32[]{:S(2)}, u32[]{:S(2)}) collective-permute-start(f32[64,256]{1,0:T(8,128)} %get-tuple-element.21), channel_id=1, source_target_pairs={{0,40},{8,41},{16,42},{24,43},{32,44},{40,45},{48,46},{56,47},{64,... | collective-permute-start | bytes 196616 | tf_op jit(solution)/shard_map/cond/branch_0_fun/ppermute | solution.py:286
  9.0 4.1 %collective-permute-start.3 = (f32[64,256]{1,0:T(8,128)}, f32[64,256]{1,0:T(8,128)S(1)}, u32[]{:S(2)}, u32[]{:S(2)}) collective-permute-start(f32[64,256]{1,0:T(8,128)} %get-tuple-element.22), channel_id=1, source_target_pairs={{0,32},{8,33},{16,34},{24,35},{32,36},{40,37},{48,38},{56,39},{64,... | collective-permute-start | bytes 196616 | tf_op jit(solution)/shard_map/cond/branch_0_fun/ppermute | solution.py:286
  9.6 4.1 %collective-permute-start.4 = (f32[64,256]{1,0:T(8,128)}, f32[64,256]{1,0:T(8,128)S(1)}, u32[]{:S(2)}, u32[]{:S(2)}) collective-permute-start(f32[64,256]{1,0:T(8,128)} %get-tuple-element.23), channel_id=1, source_target_pairs={{0,24},{8,25},{16,26},{24,27},{32,28},{40,29},{48,30},{56,31},{64,... | collective-permute-start | bytes 196616 | tf_op jit(solution)/shard_map/cond/branch_0_fun/ppermute | solution.py:286
  10.3 4.1 %collective-permute-start.5 = (f32[64,256]{1,0:T(8,128)}, f32[64,256]{1,0:T(8,128)S(1)}, u32[]{:S(2)}, u32[]{:S(2)}) collective-permute-start(f32[64,256]{1,0:T(8,128)} %get-tuple-element.24), channel_id=1, source_target_pairs={{0,16},{8,17},{16,18},{24,19},{32,20},{40,21},{48,22},{56,23},{64,... | collective-permute-start | bytes 196616 | tf_op jit(solution)/shard_map/cond/branch_0_fun/ppermute | solution.py:286
  11.0 14.8 %collective-permute-start.6 = (f32[64,256]{1,0:T(8,128)}, f32[64,256]{1,0:T(8,128)S(1)}, u32[]{:S(2)}, u32[]{:S(2)}) collective-permute-start(f32[64,256]{1,0:T(8,128)} %get-tuple-element.25), channel_id=1, source_target_pairs={{0,8},{8,9},{16,10},{24,11},{32,12},{40,13},{48,14},{56,15},{64,72... | collective-permute-start | bytes 196616 | tf_op jit(solution)/shard_map/cond/branch_0_fun/ppermute | solution.py:286
  12.3 13.5 %collective-permute-start.7 = (f32[64,256]{1,0:T(8,128)}, f32[64,256]{1,0:T(8,128)S(1)}, u32[]{:S(2)}, u32[]{:S(2)}) collective-permute-start(f32[64,256]{1,0:T(8,128)} %get-tuple-element.26), channel_id=1, source_target_pairs={{0,0},{8,1},{16,2},{24,3},{32,4},{40,5},{48,6},{56,7},{64,64},{72,... | collective-permute-start | bytes 196616 | tf_op jit(solution)/shard_map/cond/branch_0_fun/ppermute | solution.py:286
  13.0 21.2 %collective-permute-start.15 = (f32[192,128]{1,0:T(8,128)S(1)}, f32[192,128]{1,0:T(8,128)S(1)}, u32[]{:S(2)}, u32[]{:S(2)}) collective-permute-start(f32[192,128]{1,0:T(8,128)S(1)} %select_select_fusion.3), channel_id=1, source_target_pairs={{0,16},{2,18},{4,20},{6,22}} | collective-permute-start | bytes 294920 | tf_op jit(solution)/shard_map/cond/branch_0_fun/ppermute | solution.py:286
  13.7 20.6 %collective-permute-start.16 = (f32[192,128]{1,0:T(8,128)S(1)}, f32[192,128]{1,0:T(8,128)S(1)}, u32[]{:S(2)}, u32[]{:S(2)}) collective-permute-start(f32[192,128]{1,0:T(8,128)S(1)} %select_select_fusion.3), channel_id=1, source_target_pairs={{0,24},{2,26},{4,28},{6,30}} | collective-permute-start | bytes 294920 | tf_op jit(solution)/shard_map/cond/branch_0_fun/ppermute | solution.py:286
  14.4 19.9 %collective-permute-start.17 = (f32[192,128]{1,0:T(8,128)S(1)}, f32[192,128]{1,0:T(8,128)S(1)}, u32[]{:S(2)}, u32[]{:S(2)}) collective-permute-start(f32[192,128]{1,0:T(8,128)S(1)} %select_select_fusion.3), channel_id=1, source_target_pairs={{0,8},{2,10},{4,12},{6,14}} | collective-permute-start | bytes 294920 | tf_op jit(solution)/shard_map/cond/branch_0_fun/ppermute | solution.py:286
  26.7 40.8 %all-to-all-start = ((f32[8,64,256]{2,1,0:T(8,128)}), f32[8,64,256]{2,1,0:T(8,128)S(1)}, u32[]{:S(2)}, u32[]{:S(2)}) async-start(f32[8,64,256]{2,1,0:T(8,128)} %broadcast_in_dim.8), calls=%async_computation | async-start | bytes 1048576 | tf_op jit(solution)/shard_map/cond/branch_0_fun/all_to_all | solution.py:282
  34.3 55.9 %copy-start.5 = (f32[512,256]{1,0:T(8,128)S(1)}, f32[512,256]{1,0:T(8,128)}, u32[]{:S(2)}) copy-start(f32[512,256]{1,0:T(8,128)} %get-tuple-element.27) | copy-start | bytes 1572868 | tf_op jit(solution)/shard_map/cond
  34.3 10.8 %collective-permute-start.18 = (f32[192,128]{1,0:T(8,128)S(1)}, f32[192,128]{1,0:T(8,128)S(1)}, u32[]{:S(2)}, u32[]{:S(2)}) collective-permute-start(f32[192,128]{1,0:T(8,128)S(1)} %select_select_fusion.2), channel_id=1, source_target_pairs={{0,128},{2,130},{4,132},{6,134},{8,136},{10,138},{12,140},{14,142}... | collective-permute-start | bytes 294920 | tf_op jit(solution)/shard_map/cond/branch_0_fun/ppermute | solution.py:286
  45.1 6.1 %collective-permute-start.19 = (f32[192,128]{1,0:T(8,128)S(1)}, f32[192,128]{1,0:T(8,128)S(1)}, u32[]{:S(2)}, u32[]{:S(2)}) collective-permute-start(f32[192,128]{1,0:T(8,128)S(1)} %broadcast_select_fusion.1), channel_id=1, source_target_pairs={{0,64},{2,66},{4,68},{6,70},{8,72},{10,74},{12,76},{14,78},{16,80}... | collective-permute-start | bytes 294920 | tf_op jit(solution)/shard_map/cond/branch_0_fun/ppermute | solution.py:286
  46.4 6.1 %collective-permute-start.20 = (f32[192,128]{1,0:T(8,128)S(1)}, f32[192,128]{1,0:T(8,128)S(1)}, u32[]{:S(2)}, u32[]{:S(2)}) collective-permute-start(f32[192,128]{1,0:T(8,128)S(1)} %broadcast_select_fusion.1), channel_id=1, source_target_pairs={{0,224},{2,226},{4,228},{6,230},{8,232},{10,234},{12,236},{14,238}... | collective-permute-start | bytes 294920 | tf_op jit(solution)/shard_map/cond/branch_0_fun/ppermute | solution.py:286
  47.7 4.8 %collective-permute-start.21 = (f32[192,128]{1,0:T(8,128)S(1)}, f32[192,128]{1,0:T(8,128)S(1)}, u32[]{:S(2)}, u32[]{:S(2)}) collective-permute-start(f32[192,128]{1,0:T(8,128)S(1)} %broadcast_select_fusion.1), channel_id=1, source_target_pairs={{0,32},{2,34},{4,36},{6,38},{8,40},{10,42},{12,44},{14,46},{16,48}... | collective-permute-start | bytes 294920 | tf_op jit(solution)/shard_map/cond/branch_0_fun/ppermute | solution.py:286
  49.0 39.8 %collective-permute-start.8 = (f32[512,256]{1,0:T(8,128)}, f32[512,256]{1,0:T(8,128)S(1)}, u32[]{:S(2)}, u32[]{:S(2)}) collective-permute-start(f32[512,256]{1,0:T(8,128)} %get-tuple-element.27), channel_id=1, source_target_pairs={{0,4},{8,12},{16,20},{24,28},{32,36},{40,44},{48,52},{56,60},{64,6... | collective-permute-start | bytes 1572872 | tf_op jit(solution)/shard_map/cond/branch_0_fun/ppermute | solution.py:286
  49.7 40.4 %collective-permute-start.9 = (f32[512,256]{1,0:T(8,128)}, f32[512,256]{1,0:T(8,128)}, u32[]{:S(2)}, u32[]{:S(2)}) collective-permute-start(f32[512,256]{1,0:T(8,128)} %get-tuple-element.27), channel_id=1, source_target_pairs={{0,6},{8,14},{16,22},{24,30},{32,38},{40,46},{48,54},{56,62},{64,7... | collective-permute-start | bytes 1572872 | tf_op jit(solution)/shard_map/cond/branch_0_fun/ppermute | solution.py:286
  51.2 38.9 %collective-permute-start.10 = (f32[512,256]{1,0:T(8,128)}, f32[512,256]{1,0:T(8,128)}, u32[]{:S(2)}, u32[]{:S(2)}) collective-permute-start(f32[512,256]{1,0:T(8,128)} %get-tuple-element.27), channel_id=1, source_target_pairs={{0,2},{8,10},{16,18},{24,26},{32,34},{40,42},{48,50},{56,58},{64,6... | collective-permute-start | bytes 1572872 | tf_op jit(solution)/shard_map/cond/branch_0_fun/ppermute | solution.py:286
  52.6 25.0 %collective-permute-start.22 = (f32[192,128]{1,0:T(8,128)S(1)}, f32[192,128]{1,0:T(8,128)}, u32[]{:S(2)}, u32[]{:S(2)}) collective-permute-start(f32[192,128]{1,0:T(8,128)S(1)} %select_select_fusion.1), channel_id=1, source_target_pairs={{0,1},{2,3},{4,5},{6,7},{8,9},{10,11},{12,13},{14,15},{16,17},{18,... | collective-permute-start | bytes 294920 | tf_op jit(solution)/shard_map/cond/branch_0_fun/ppermute | solution.py:286
  54.5 25.0 %collective-permute-start.23 = (f32[192,128]{1,0:T(8,128)S(1)}, f32[192,128]{1,0:T(8,128)S(1)}, u32[]{:S(2)}, u32[]{:S(2)}) collective-permute-start(f32[192,128]{1,0:T(8,128)S(1)} %select_select_fusion.1), channel_id=1, source_target_pairs={{2,0},{4,2},{6,4},{0,6},{10,8},{12,10},{14,12},{8,14},{18,16},{20,... | collective-permute-start | bytes 294920 | tf_op jit(solution)/shard_map/cond/branch_0_fun/ppermute | solution.py:286
  69.1 41.3 %copy-start.3 = (s32[64,64]{1,0:T(8,128)S(1)}, s32[64,64]{1,0:T(8,128)}, u32[]{:S(2)}) copy-start(s32[64,64]{1,0:T(8,128)} %get-tuple-element.17.map_ref) | copy-start | bytes 49156 | tf_op jit(solution)/shard_map/cond
  69.1 40.0 %all-to-all-start.1 = ((f32[4,8,64,256]{3,2,1,0:T(8,128)}), f32[4,8,64,256]{3,2,1,0:T(8,128)S(1)}, u32[]{:S(2)}, u32[]{:S(2)}) async-start(f32[4,8,64,256]{3,2,1,0:T(8,128)} %broadcast_in_dim.9), calls=%async_computation.1 | async-start | bytes 4194304 | tf_op jit(solution)/shard_map/cond/branch_0_fun/all_to_all | solution.py:282
  77.6 6.6 %collective-permute-start.25 = (f32[192,128]{1,0:T(8,128)S(1)}, f32[192,128]{1,0:T(8,128)S(1)}, u32[]{:S(2)}, u32[]{:S(2)}) collective-permute-start(f32[192,128]{1,0:T(8,128)S(1)} %select_select_fusion.1), channel_id=1, source_target_pairs={{6,0},{0,2},{2,4},{4,6},{14,8},{8,10},{10,12},{12,14},{22,16},{16,... | collective-permute-start | bytes 294920 | tf_op jit(solution)/shard_map/cond/branch_0_fun/ppermute | solution.py:286
  79.5 8.0 %collective-permute-start.27 = (f32[192,128]{1,0:T(8,128)S(1)}, f32[192,128]{1,0:T(8,128)S(1)}, u32[]{:S(2)}, u32[]{:S(2)}) collective-permute-start(f32[192,128]{1,0:T(8,128)S(1)} %select_select_fusion.1), channel_id=1, source_target_pairs={{4,0},{6,2},{0,4},{2,6},{12,8},{14,10},{8,12},{10,14},{20,16},{22,... | collective-permute-start | bytes 294920 | tf_op jit(solution)/shard_map/cond/branch_0_fun/ppermute | solution.py:286
  84.2 8.7 %collective-permute-start.24 = (f32[192,128]{1,0:T(8,128)S(1)}, f32[192,128]{1,0:T(8,128)S(1)}, u32[]{:S(2)}, u32[]{:S(2)}) collective-permute-start(f32[192,128]{1,0:T(8,128)S(1)} %collective-permute-done.23), channel_id=1, source_target_pairs={{0,1},{2,3},{4,5},{6,7},{8,9},{10,11},{12,13},{14,15},{16,17},{18,... | collective-permute-start | bytes 294920 | tf_op jit(solution)/shard_map/cond/branch_0_fun/ppermute | solution.py:286
  87.5 6.0 %collective-permute-start.26 = (f32[192,128]{1,0:T(8,128)S(1)}, f32[192,128]{1,0:T(8,128)S(1)}, u32[]{:S(2)}, u32[]{:S(2)}) collective-permute-start(f32[192,128]{1,0:T(8,128)S(1)} %collective-permute-done.25), channel_id=1, source_target_pairs={{0,1},{2,3},{4,5},{6,7},{8,9},{10,11},{12,13},{14,15},{16,17},{18,... | collective-permute-start | bytes 294920 | tf_op jit(solution)/shard_map/cond/branch_0_fun/ppermute | solution.py:286
  88.8 1.3 %copy-start.6 = (f32[512,256]{1,0:T(8,128)}, f32[512,256]{1,0:T(8,128)S(1)}, u32[]{:S(2)}) copy-start(f32[512,256]{1,0:T(8,128)S(1)} %collective-permute-done.8) | copy-start | bytes 1572868 | tf_op jit(solution)/shard_map/cond
  88.9 5.4 %collective-permute-start.28 = (f32[192,128]{1,0:T(8,128)S(1)}, f32[192,128]{1,0:T(8,128)S(1)}, u32[]{:S(2)}, u32[]{:S(2)}) collective-permute-start(f32[192,128]{1,0:T(8,128)S(1)} %collective-permute-done.27), channel_id=1, source_target_pairs={{0,1},{2,3},{4,5},{6,7},{8,9},{10,11},{12,13},{14,15},{16,17},{18,... | collective-permute-start | bytes 294920 | tf_op jit(solution)/shard_map/cond/branch_0_fun/ppermute | solution.py:286
  91.4 16.8 %collective-permute-start.11 = (f32[512,256]{1,0:T(8,128)S(1)}, f32[512,256]{1,0:T(8,128)S(1)}, u32[]{:S(2)}, u32[]{:S(2)}) collective-permute-start(f32[512,256]{1,0:T(8,128)S(1)} %select_select_fusion), channel_id=1, source_target_pairs={{0,1},{2,3},{4,5},{6,7},{8,9},{10,11},{12,13},{14,15},{16,17},{18,... | collective-permute-start | bytes 1572872 | tf_op jit(solution)/shard_map/cond/branch_0_fun/ppermute | solution.py:286
  109.1 1.3 %copy-start = (f32[4,8,64,256]{3,2,1,0:T(8,128)}, f32[4,8,64,256]{3,2,1,0:T(8,128)S(1)}, u32[]{:S(2)}) copy-start(f32[4,8,64,256]{3,2,1,0:T(8,128)S(1)} %all-to-all-done.1) | copy-start | bytes 6291460 | tf_op jit(solution)/shard_map/cond
